TPU v7x, 512 devices: a whole 4x4x16 slice. The times are simulated.
512 devices in a mesh: region: 32 (over x, z_lo), run: 16 (over z_hi, y, core).
Axes of the slice: x: 4, y: 4, z: 16 (z_hi: 2, z_lo: 8; z = z_hi * 8 + z_lo), core: 2. Of those that a mesh axis runs over, the one named last changes fastest.
Arguments:
- sensitivity: bfloat16 [12288, 65536], P('run', 'region'), may hold values from -0.75 to 0.75
- run_counts: int32 [512], P('region'), may hold values from 768 to 3072
- req_owner: int32 [1024, 1], P('region'), may hold values from 0 to 31; in each aligned block of 32 rows (0 to 31, 32 to 63, ...) no two rows name the same one
- req_block: int32 [1024], P('region'), may hold values from 0 to 15
- coupled: int32 [1024, 2], P('region'), may hold values from 0 to 15, all different within a row
Outputs:
- fisher: bfloat16 [1024, 2, 128, 128], P('region', None, 'run')
- mirror: bfloat16 [32, 32, 1, 2, 128, 128], P('region', None, None, None, None, 'run')
Inputs may be any that keep to these rules, and one draw needn't show every extreme that they name: `req_owner`: among the requests of one region device every owner is named exactly 1 times. `coupled`: the 2 local blocks of one request differ.
All inputs are finite; a program needn't handle non-finite values.
Results may differ from a plain program's by a relative error of at most 0.001.
Values may be sent and summed in bfloat16 or wider, within the bound.
A program may use at most 128 MiB of HBM per device.

v0:
```python
import jax
import jax.numpy as jnp
from jax import lax
from jax.sharding import PartitionSpec as P

OBS = 4
COUPLE = 2
CAP = 1


def shards(sensitivity, run_counts, req_owner, req_block, coupled):
    regions = lax.axis_size("region")
    rows_dev = sensitivity.shape[0]
    blocks = run_counts.shape[0]
    block_width = sensitivity.shape[1] // blocks
    requests = req_owner.shape[0]
    slot_count = regions * CAP
    first_run = lax.axis_index("run") * (rows_dev // OBS)
    row_run = first_run + jnp.arange(rows_dev, dtype=jnp.int32) // OBS
    live_mask = row_run[:, None] < run_counts[None, :]
    shaped = sensitivity.reshape(rows_dev, blocks, block_width)
    masked = jnp.where(live_mask[:, :, None], shaped, jnp.zeros((), jnp.bfloat16))
    owner_of = req_owner[:, 0]
    ordinal = jnp.arange(requests, dtype=jnp.int32)
    earlier = (owner_of[:, None] == owner_of[None, :]) & (ordinal[None, :] < ordinal[:, None])
    position = jnp.sum(earlier.astype(jnp.int32), axis=1)
    slot_of = owner_of * CAP + position
    picker = slot_of[:, None] == jnp.arange(slot_count, dtype=jnp.int32)[None, :]
    wanted = jnp.sum(jnp.where(picker, req_block[:, None] + 1, 0), axis=0) - 1
    asked = lax.all_to_all(
        wanted.reshape(regions, CAP), "region", split_axis=0, concat_axis=0, tiled=True
    ).reshape(slot_count)
    outgoing = jnp.take(masked, jnp.maximum(asked, 0), axis=1)
    outgoing = jnp.where((asked >= 0)[None, :, None], outgoing, jnp.zeros((), jnp.bfloat16))
    arrived = lax.all_to_all(outgoing, "region", split_axis=1, concat_axis=1, tiled=True)
    remote = jnp.take(arrived, slot_of, axis=1)
    local_cols = jnp.take(masked, coupled.reshape(-1), axis=1).reshape(
        rows_dev, requests, COUPLE, block_width
    )
    partial_value = jnp.einsum(
        "rkcm,rkn->kcmn", local_cols, remote, preferred_element_type=jnp.float32
    )
    whole_sum = lax.psum(partial_value, "run")
    share = whole_sum.shape[2] // lax.axis_size("run")
    summed = lax.dynamic_slice_in_dim(whole_sum, lax.axis_index("run") * share, share, 2)
    fisher = summed.astype(jnp.bfloat16)
    flipped = jnp.swapaxes(fisher, 2, 3)
    placed = jnp.einsum(
        "ks,kcmn->scmn", picker.astype(jnp.bfloat16), flipped, preferred_element_type=jnp.float32
    )
    placed = placed.astype(jnp.bfloat16).reshape(
        regions, CAP, COUPLE, block_width, flipped.shape[3]
    )
    returned = lax.all_to_all(placed, "region", split_axis=0, concat_axis=0, tiled=True)
    mirror = returned[None]
    return (fisher, mirror)


def solution(mesh):
    in_specs = (P("run", "region"), P("region"), P("region", None), P("region"), P("region", None))
    out_specs = (P("region", None, "run", None), P("region", None, None, None, None, "run"))
    return jax.shard_map(shards, mesh=mesh, in_specs=in_specs, out_specs=out_specs, check_vma=False)
```

profile of v0, /device:TPU:2, one launch (start us, length us, event | category | flops | bytes accessed | tf_op | source)
XLA Modules:
  0.0 594.8 jit_solution(14731809041079875929)
XLA Ops:
  0.6 0.7 broadcast_add_fusion
  1.3 0.9 convert_reduce_fusion
  2.2 0.7 fusion.19
  2.9 0.1 select_reduce_fusion
  3.0 0.7 copy.47
  3.7 15.7 %all-to-all-start = ((s32[32,1,1]{2,1,0:T(1,128)}), s32[32,1,1]{2,1,0:T(1,128)S(1)}, u32[]{:S(2)}, u32[]{:S(2)}) async-start(s32[32,1,1]{2,1,0:T(1,128)} %copy.47), calls=%async_computation | async-start | bytes 32768 | tf_op jit(solution)/shard_map/all_to_all | solution.py:30
  19.4 0.0 copy-start.1
  19.4 3.2 copy.43
  22.6 2.8 copy.44
  25.4 0.0 copy-done.1
  25.4 0.1 broadcast_compare_fusion
  25.5 5.8 broadcast_select_fusion
  31.3 0.0 all-to-all-done
  31.3 0.7 maximum_reduce_fusion
  32.0 4.1 gather_fusion.1
  36.0 1.2 compare_reduce_fusion
  37.3 6.3 %select_bitcast_fusion = bf16[768,32,128]{2,0,1:T(8,128)(2,1)} fusion(bf16[32,768,128]{2,1,0:T(8,128)(2,1)} %gather_fusion.1, pred[32]{0:T(512)(128)(4,1)S(1)} %get-tuple-element.15, pred[32]{0:T(512)(128)(4,1)S(1)} %get-tuple-element.14), kind=kLoop, calls=%fused_computation.7 | loop fusion | flops 6291456 | bytes 12582976 | tf_op jit(solution)/shard_map/jit(_where)/select_n | solution.py:34
  43.5 0.0 copy-start
  43.5 12.7 %all-to-all-start.1 = ((bf16[768,32,128]{2,0,1:T(8,128)(2,1)}), bf16[768,32,128]{2,0,1:T(8,128)(2,1)}, u32[]{:S(2)}, u32[]{:S(2)}) async-start(bf16[768,32,128]{2,0,1:T(8,128)(2,1)} %select_bitcast_fusion), calls=%async_computation.1 | async-start | bytes 12582912 | tf_op jit(solution)/shard_map/all_to_all | solution.py:35
  56.2 0.0 copy-done
  56.2 0.1 copy.45
  56.3 0.1 reshape.143
  56.4 7.2 %gather_fusion = bf16[64,768,128]{2,1,0:T(8,128)(2,1)} fusion(bf16[768,16,128]{2,0,1:T(8,128)(2,1)S(1)} %broadcast_select_fusion, s32[1024]{0:T(1024)S(1)} %pad_clamp_fusion.2), kind=kCustom, calls=%fused_computation | custom fusion | bytes 25166080 | tf_op jit(solution)/shard_map/jit(_take)/gather | solution.py:37
  63.7 0.0 copy-start.2
  63.7 16.6 %copy.46 = bf16[768,32,2,128]{0,3,2,1:T(8,128)(2,1)} copy(bf16[768,32,2,128]{3,0,2,1:T(8,128)(2,1)} %bitcast.42) | data formatting | bytes 25165824 | tf_op jit(solution)/shard_map/jit(_take)/gather | solution.py:37
  80.3 0.1 copy.42
  80.4 0.0 copy-done.2
  80.4 237.0 %all-to-all-done.1 = bf16[768,32,128]{2,0,1:T(8,128)(2,1)} async-done(((bf16[768,32,128]{2,0,1:T(8,128)(2,1)}), bf16[768,32,128]{2,0,1:T(8,128)(2,1)}, u32[]{:S(2)}, u32[]{:S(2)}) %all-to-all-start.1) | async-done | bytes 6291488 | tf_op jit(solution)/shard_map/all_to_all | solution.py:35
  317.4 6.7 %gather_fusion.2 = bf16[32,768,128]{2,1,0:T(8,128)(2,1)} fusion(bf16[768,32,128]{2,0,1:T(8,128)(2,1)} %all-to-all-done.1, s32[1024]{0:T(1024)S(1)} %pad_clamp_fusion), kind=kCustom, calls=%fused_computation.2 | custom fusion | bytes 12583040 | tf_op jit(solution)/shard_map/jit(_take)/gather | solution.py:36
  324.1 11.9 %fusion = f32[32,2,128,128]{3,2,1,0:T(8,128)} fusion(bf16[768,32,2,128]{0,3,2,1:T(8,128)(2,1)} %copy.46, pred[32,2]{1,0:T(8,128)(4,1)S(1)} %copy.42, bf16[32,768,128]{2,1,0:T(8,128)(2,1)} %gather_fusion.2, pred[32]{0:T(512)(128)(4,1)S(1)} %get-tuple-element.16), kind=kOutput, calls=%fused_computation.3 | convolution fusion | flops 1620049920 | bytes 23068768 | tf_op jit(solution)/shard_map/rkcm,rkn->kcmn/dot_general | solution.py:40
  336.1 225.4 %all-reduce.1 = bf16[32,2,128,128]{3,2,1,0:T(8,128)(2,1)S(1)} all-reduce(f32[32,2,128,128]{3,2,1,0:T(8,128)} %fusion), channel_id=1, replica_groups=mesh['region'=32,'run'=16] {'run'}, use_global_device_ids=true, to_apply=%region_2.3 | all-reduce | flops 1048576 | bytes 6291456 | tf_op jit(solution)/shard_map/psum | solution.py:43
  561.5 0.2 fusion.8
  561.7 0.7 copy.49
  562.4 19.9 %all-to-all-start.2 = ((bf16[32,1,2,128,8]{3,4,2,1,0:T(8,128)(2,1)}), bf16[32,1,2,128,8]{3,4,2,1,0:T(8,128)(2,1)S(1)}, u32[]{:S(2)}, u32[]{:S(2)}) async-start(bf16[32,1,2,128,8]{3,4,2,1,0:T(8,128)(2,1)} %copy.49), calls=%async_computation.2 | async-start | bytes 262144 | tf_op jit(solution)/shard_map/all_to_all | solution.py:54
  582.3 0.7 dynamic-slice_convert_fusion
  583.0 11.1 %all-to-all-done.2 = bf16[32,1,2,128,8]{3,4,2,1,0:T(8,128)(2,1)S(1)} async-done(((bf16[32,1,2,128,8]{3,4,2,1,0:T(8,128)(2,1)}), bf16[32,1,2,128,8]{3,4,2,1,0:T(8,128)(2,1)S(1)}, u32[]{:S(2)}, u32[]{:S(2)}) %all-to-all-start.2) | async-done | bytes 131104 | tf_op jit(solution)/shard_map/all_to_all | solution.py:54
  594.1 0.7 copy.58
  (9 shorter events, 0.1 us)
Async XLA Ops:
  3.7 27.6 %all-to-all-start = ((s32[32,1,1]{2,1,0:T(1,128)}), s32[32,1,1]{2,1,0:T(1,128)S(1)}, u32[]{:S(2)}, u32[]{:S(2)}) async-start(s32[32,1,1]{2,1,0:T(1,128)} %copy.47), calls=%async_computation | async-start | bytes 32768 | tf_op jit(solution)/shard_map/all_to_all | solution.py:30
  19.4 6.0 %copy-start.1 = (s32[16]{0:T(128)S(1)}, s32[16]{0:T(128)}, u32[]{:S(2)}) copy-start(s32[16]{0:T(128)} %param.6) | copy-start | bytes 196
  43.5 12.7 %copy-start = (s32[32,2]{0,1:T(2,128)S(1)}, s32[32,2]{0,1:T(2,128)}, u32[]{:S(2)}) copy-start(s32[32,2]{0,1:T(2,128)} %param.9) | copy-start | bytes 772
  43.5 273.9 %all-to-all-start.1 = ((bf16[768,32,128]{2,0,1:T(8,128)(2,1)}), bf16[768,32,128]{2,0,1:T(8,128)(2,1)}, u32[]{:S(2)}, u32[]{:S(2)}) async-start(bf16[768,32,128]{2,0,1:T(8,128)(2,1)} %select_bitcast_fusion), calls=%async_computation.1 | async-start | bytes 12582912 | tf_op jit(solution)/shard_map/all_to_all | solution.py:35
  63.7 16.7 %copy-start.2 = (s32[32,1]{0,1:T(1,128)S(1)}, s32[32,1]{0,1:T(1,128)}, u32[]{:S(2)}) copy-start(s32[32,1]{0,1:T(1,128)} %param.7) | copy-start | bytes 388
  562.4 31.7 %all-to-all-start.2 = ((bf16[32,1,2,128,8]{3,4,2,1,0:T(8,128)(2,1)}), bf16[32,1,2,128,8]{3,4,2,1,0:T(8,128)(2,1)S(1)}, u32[]{:S(2)}, u32[]{:S(2)}) async-start(bf16[32,1,2,128,8]{3,4,2,1,0:T(8,128)(2,1)} %copy.49), calls=%async_computation.2 | async-start | bytes 262144 | tf_op jit(solution)/shard_map/all_to_all | solution.py:54
where the time goes:
time: 596 us; the launch traced here: 595 us
  waiting for transfers between devices  248 us (42%)
  blocking collectives  225 us (38%)
  starting transfers between devices  48.3 us (8%)
  local copies, waits for them, and re-layouts  43.8 us (7%)
  other arithmetic  16.4 us (3%)
  matrix products  12.1 us (2%)
    all_to_all x1, waiting for transfers between devices, shards(): lax.all_to_all(outgoing, 'region', split_axis=1, concat_axis=1, tiled=True)  237 us
    psum x1, blocking collectives, shards(): whole_sum = lax.psum(partial_value, 'run')  225 us
    gather x2, local copies, waits for them, and re-layouts, shards(): jnp.take(masked, coupled.reshape(-1), axis=1)  23.9 us
    all_to_all x1, starting transfers between devices, shards(): lax.all_to_all(placed, 'region', split_axis=0, concat_axis=0, tiled=True)  19.9 us
    all_to_all x1, starting transfers between devices, shards(): lax.all_to_all(wanted.reshape(regions, CAP), 'region', split_axis=0, conc...  15.7 us
    all_to_all x1, starting transfers between devices, shards(): lax.all_to_all(outgoing, 'region', split_axis=1, concat_axis=1, tiled=True)  12.7 us
  transfers between devices with their start and end apart: 3, of which 2 were waited for; matrix products, arithmetic and copies ran while one was open for 6% of the time, Pallas kernels for 0%

commit v1 on v0

v1 whole, which is shorter than its diff:
```python
import jax
import jax.numpy as jnp
from jax import lax
from jax.sharding import Mesh, PartitionSpec as P

OBS = 4
COUPLE = 2
BS = 128
PLANE = ("x", "y", "core")
REGION = ("x", "zlo")
RUN = ("zhi", "y", "core")


def shards(sensitivity, run_counts, req_owner, req_block, coupled):
    rows_dev = sensitivity.shape[0]
    blocks = run_counts.shape[0]
    requests = req_owner.shape[0]
    regions = lax.axis_size(REGION)
    zlo = lax.axis_size("zlo")
    runs = lax.axis_size(RUN)
    chunk = rows_dev // zlo
    mine = lax.axis_index(PLANE)

    table = jnp.concatenate([req_owner, req_block[:, None], coupled], axis=1)
    tables = lax.all_gather(table, REGION, axis=0, tiled=False)

    first_run = lax.axis_index(RUN) * (rows_dev // OBS)
    row_run = first_run + jnp.arange(rows_dev, dtype=jnp.int32) // OBS
    counts = jnp.repeat(run_counts, BS)
    masked = jnp.where(row_run[:, None] < counts[None, :], sensitivity, jnp.zeros((), jnp.bfloat16))
    part = lax.all_to_all(masked.reshape(zlo, chunk, blocks * BS), "zlo", 0, 0, tiled=True)
    part = lax.all_to_all(part, ("y", "core"), 0, 0, tiled=True)
    local = part.reshape(rows_dev, blocks, BS)

    asked = jnp.sum(jnp.where(tables[:, :, 0] == mine, tables[:, :, 1], 0), axis=1)
    outgoing = jnp.transpose(jnp.take(local, asked, axis=1), (1, 0, 2))
    arrived = lax.all_to_all(outgoing, PLANE, 0, 0, tiled=True)

    own = lax.dynamic_index_in_dim(tables, mine, 0, keepdims=False)
    hit = own[:, 0][None, :] == jnp.arange(regions, dtype=jnp.int32)[:, None]
    near = jnp.sum(jnp.where(hit[:, :, None], own[None, :, 2:], 0), axis=1)
    local_cols = jnp.take(local, near.reshape(-1), axis=1).reshape(rows_dev, regions, COUPLE, BS)
    partial_value = jnp.einsum(
        "rkcm,krn->mkcn", local_cols, arrived, preferred_element_type=jnp.float32
    )
    summed = lax.psum_scatter(partial_value, ("zhi", "zlo"), scatter_dimension=0, tiled=True)
    held = summed.astype(jnp.bfloat16)

    ny = lax.axis_size("y")
    nc = lax.axis_size("core")
    pairs = []
    for a in range(zlo):
        for y in range(ny):
            for c in range(nc):
                pairs.append(((a * ny + y) * nc + c, ((y * nc + c) * ny + a // nc) * nc + a % nc))
    slices = lax.ppermute(held, ("zlo", "y", "core"), pairs)
    mslice = slices.shape[0]
    by_owner = jnp.transpose(slices, (1, 2, 0, 3))
    fisher = jnp.take(by_owner, req_owner[:, 0], axis=0)
    placed = jnp.transpose(slices, (1, 2, 3, 0))
    returned = lax.all_to_all(placed, REGION, 0, 0, tiled=True)
    return fisher, returned.reshape(1, regions, 1, COUPLE, BS, mslice)


def solution(mesh):
    fine = Mesh(mesh.devices.reshape(4, 8, 2, 4, 2), ("x", "zlo", "zhi", "y", "core"))
    in_specs = (P(RUN, REGION), P(REGION), P(REGION, None), P(REGION), P(REGION, None))
    out_specs = (P(REGION, None, RUN, None), P(REGION, None, None, None, None, RUN))
    return jax.shard_map(shards, mesh=fine, in_specs=in_specs, out_specs=out_specs, check_vma=False)
```

time: 596 us -> 542 us (0.909)
  the two profiles are of different devices: /device:TPU:2 before, /device:TPU:1 now
where the time goes in v1:
time: 542 us; the launch traced here: 534 us
  blocking collectives  256 us (47%)
  waiting for transfers between devices  157 us (29%)
  starting transfers between devices  53.6 us (10%)
  local copies, waits for them, and re-layouts  30.5 us (6%)
  between operations  14.3 us (3%)
  other arithmetic  11.3 us (2%)
  matrix products  10.9 us (2%)
    all_to_all x1, blocking collectives, shards(): lax.all_to_all(masked.reshape(zlo, chunk, blocks * BS), 'zlo', 0, 0, tile...  153 us
    all_gather x1, blocking collectives, shards(): tables = lax.all_gather(table, REGION, axis=0, tiled=False)  103 us
    reduce_scatter x1, waiting for transfers between devices, shards(): lax.psum_scatter(partial_value, ('zhi', 'zlo'), scatter_dimension=0, tile...  73.9 us
    all_to_all x1, waiting for transfers between devices, shards(): arrived = lax.all_to_all(outgoing, PLANE, 0, 0, tiled=True)  70.1 us
    all_to_all x1, starting transfers between devices, shards(): arrived = lax.all_to_all(outgoing, PLANE, 0, 0, tiled=True)  19.1 us
    all_to_all x1, starting transfers between devices, shards(): returned = lax.all_to_all(placed, REGION, 0, 0, tiled=True)  14.9 us
    ppermute x1, starting transfers between devices, shards(): slices = lax.ppermute(held, ('zlo', 'y', 'core'), pairs)  13.3 us
    gather x2, local copies, waits for them, and re-layouts, shards(): outgoing = jnp.transpose(jnp.take(local, asked, axis=1), (1, 0, 2))  12.7 us
  transfers between devices with their start and end apart: 5, of which 4 were waited for; matrix products, arithmetic and copies ran while one was open for 2% of the time, Pallas kernels for 0%

profile of v1, /device:TPU:1, one launch (start us, length us, event | category | flops | bytes accessed | tf_op | source)
XLA Modules:
  0.0 533.7 jit_solution(8117074581794383060)
XLA Ops:
  7.2 0.0 copy-start
  7.2 0.6 copy-done
  7.8 0.1 broadcast_bitcast_fusion
  7.9 2.7 compare_select_fusion
  10.6 0.0 copy-start.1
  10.6 0.0 copy-start.2
  10.6 0.0 copy-start.3
  10.6 153.3 %all_to_all.20 = bf16[8,96,2048]{2,1,0:T(8,128)(2,1)} all-to-all(bf16[8,96,2048]{2,1,0:T(8,128)(2,1)S(1)} %bitcast.44), channel_id=1, replica_groups=mesh['x'=4,'zlo'=8,'zhi'=2,'y'=4,'core'=2] {'zlo'}, dimensions={0} | all-to-all | bytes 6291456 | tf_op jit(solution)/shard_map/all_to_all | solution.py:31
  163.9 6.3 %all-to-all-start.1 = ((bf16[8,96,2048]{2,1,0:T(8,128)(2,1)}), bf16[8,96,2048]{2,1,0:T(8,128)(2,1)S(1)}, u32[]{:S(2)}, u32[]{:S(2)}) async-start(bf16[8,96,2048]{2,1,0:T(8,128)(2,1)} %all_to_all.20), calls=%async_computation.1 | async-start | bytes 6291456 | tf_op jit(solution)/shard_map/all_to_all | solution.py:32
  170.2 0.0 copy-done.1
  170.2 0.0 copy-done.2
  170.2 0.0 copy-done.3
  170.3 102.8 %all-gather.1 = s32[32,32,4]{1,2,0:T(4,128)S(1)} all-gather(s32[1,32,4]{1,2,0:T(4,128)S(1)} %add_bitcast_fusion), channel_id=2, replica_groups=mesh['x'=4,'zlo'=8,'zhi'=2,'y'=4,'core'=2] {'x','zlo'}, dimensions={0}, use_global_device_ids=true | all-gather | bytes 16896 | tf_op jit(solution)/shard_map/all_gather | solution.py:25
  273.0 0.7 fusion.10
  273.7 0.0 all-to-all-done.1
  273.7 1.0 copy.46
  274.7 0.8 copy.36
  275.6 4.0 gather_fusion
  279.6 8.7 %copy.37 = bf16[32,768,128]{1,2,0:T(8,128)(2,1)} copy(bf16[32,768,128]{2,1,0:T(8,128)(2,1)} %gather_fusion) | data formatting | bytes 12582912 | tf_op jit(solution)/shard_map/jit(_take)/gather | solution.py:36
  288.3 6.1 %broadcast_select_fusion = bf16[32,768,128]{1,2,0:T(8,128)(2,1)} fusion(bf16[32,768,128]{1,2,0:T(8,128)(2,1)} %copy.37, pred[32]{0:T(512)(128)(4,1)S(1)} %compare_and_fusion.1), kind=kLoop, calls=%fused_computation.8 | loop fusion | flops 3145728 | bytes 12582944 | tf_op jit(solution)/shard_map/jit(_take)/select_n | solution.py:36
  294.3 19.1 %all-to-all-start.2 = ((bf16[32,768,128]{1,2,0:T(8,128)(2,1)}), bf16[32,768,128]{1,2,0:T(8,128)(2,1)}, u32[]{:S(2)}, u32[]{:S(2)}) async-start(bf16[32,768,128]{1,2,0:T(8,128)(2,1)} %broadcast_select_fusion), calls=%async_computation.2 | async-start | bytes 12582912 | tf_op jit(solution)/shard_map/all_to_all | solution.py:37
  313.4 0.0 reduce-scatter.2.cloned.1.call-start
  313.5 0.1 select_reduce_fusion
  313.6 0.1 copy.39
  313.7 0.1 copy.38
  313.8 0.1 reshape.117
  314.0 7.3 %gather_fusion.1 = bf16[64,768,128]{2,1,0:T(8,128)(2,1)} fusion(bf16[768,16,128]{2,0,1:T(8,128)(2,1)S(1)} %copy.36, s32[1024]{0:T(1024)S(1)} %pad_clamp_fusion.1), kind=kCustom, calls=%fused_computation.1 | custom fusion | bytes 25166080 | tf_op jit(solution)/shard_map/jit(_take)/gather | solution.py:42
  321.3 70.1 %all-to-all-done.2 = bf16[32,768,128]{1,2,0:T(8,128)(2,1)} async-done(((bf16[32,768,128]{1,2,0:T(8,128)(2,1)}), bf16[32,768,128]{1,2,0:T(8,128)(2,1)}, u32[]{:S(2)}, u32[]{:S(2)}) %all-to-all-start.2) | async-done | bytes 6291488 | tf_op jit(solution)/shard_map/all_to_all | solution.py:37
  391.4 10.9 %fusion.5 = f32[128,32,2,128]{0,3,2,1:T(8,128)} fusion(bf16[768,32,2,128]{3,0,2,1:T(8,128)(2,1)} %bitcast.45, pred[32,2]{1,0:T(8,128)(4,1)S(1)} %copy.38, bf16[32,768,128]{1,2,0:T(8,128)(2,1)} %all-to-all-done.2), kind=kOutput, calls=%fused_computation.10 | convolution fusion | flops 1616904192 | bytes 23068736 | tf_op jit(solution)/shard_map/rkcm,krn->mkcn/dot_general | solution.py:43
  402.3 5.5 %copy.41 = f32[128,32,2,128]{3,1,2,0:T(8,128)} copy(f32[128,32,2,128]{0,3,2,1:T(8,128)} %fusion.5) | data formatting | bytes 8388608 | tf_op jit(solution)/shard_map/rkcm,krn->mkcn/transpose | solution.py:43
  407.8 0.0 reduce-scatter.2.cloned.1.call-update
  407.9 73.9 %reduce-scatter.2.cloned.1.call-done = f32[8,32,2,128]{3,1,2,0:T(8,128)} async-done(((f32[128,32,2,128]{3,1,2,0:T(8,128)}), f32[8,32,2,128]{3,1,2,0:T(8,128)}) %reduce-scatter.2.cloned.1.call-update) | async-done | bytes 262160 | tf_op jit(solution)/shard_map/reduce_scatter | solution.py:46
  481.7 1.0 convert_element_type.3
  482.7 13.3 %collective-permute-start = (bf16[8,32,2,128]{3,1,2,0:T(8,128)(2,1)S(1)}, bf16[8,32,2,128]{3,1,2,0:T(8,128)(2,1)S(1)}, u32[]{:S(2)}, u32[]{:S(2)}) collective-permute-start(bf16[8,32,2,128]{3,1,2,0:T(8,128)(2,1)S(1)} %convert_element_type.3), channel_id=1, source_target_pairs={{0,0},{1,16},{2,32},{3,48},{4,64},{5,80},{6,96},{7,112},{16,1},{17... | collective-permute-start | bytes 393224 | tf_op jit(solution)/shard_map/ppermute | solution.py:56
  496.1 2.6 collective-permute-done
  498.7 0.7 copy.43
  499.5 14.9 %all-to-all-start.3 = ((bf16[32,2,128,8]{2,3,1,0:T(8,128)(2,1)}), bf16[32,2,128,8]{2,3,1,0:T(8,128)(2,1)S(1)}, u32[]{:S(2)}, u32[]{:S(2)}) async-start(bf16[32,2,128,8]{2,3,1,0:T(8,128)(2,1)} %copy.43), calls=%async_computation.4 | async-start | bytes 262144 | tf_op jit(solution)/shard_map/all_to_all | solution.py:61
  514.4 0.1 copy.48
  514.5 0.6 gather_fusion.2
  515.0 0.8 broadcast_select_fusion.1
  515.8 10.4 %all-to-all-done.3 = bf16[32,2,128,8]{2,3,1,0:T(8,128)(2,1)S(1)} async-done(((bf16[32,2,128,8]{2,3,1,0:T(8,128)(2,1)}), bf16[32,2,128,8]{2,3,1,0:T(8,128)(2,1)S(1)}, u32[]{:S(2)}, u32[]{:S(2)}) %all-to-all-start.3) | async-done | bytes 131104 | tf_op jit(solution)/shard_map/all_to_all | solution.py:61
  526.2 0.7 copy.50
  (15 shorter events, 0.1 us)
Async XLA Ops:
  7.2 0.7 copy-start
  10.6 159.7 %copy-start.1 = (s32[32,2]{0,1:T(2,128)S(1)}, s32[32,2]{0,1:T(2,128)}, u32[]{:S(2)}) copy-start(s32[32,2]{0,1:T(2,128)} %param.9) | copy-start | bytes 772
  10.6 159.6 %copy-start.2 = (s32[32]{0:T(128)S(1)}, s32[32]{0:T(128)}, u32[]{:S(2)}) copy-start(s32[32]{0:T(128)} %param.8) | copy-start | bytes 388
  10.6 159.6 %copy-start.3 = (s32[32,1]{0,1:T(1,128)S(1)}, s32[32,1]{0,1:T(1,128)}, u32[]{:S(2)}) copy-start(s32[32,1]{0,1:T(1,128)} %param.7) | copy-start | bytes 388
  163.9 109.8 %all-to-all-start.1 = ((bf16[8,96,2048]{2,1,0:T(8,128)(2,1)}), bf16[8,96,2048]{2,1,0:T(8,128)(2,1)S(1)}, u32[]{:S(2)}, u32[]{:S(2)}) async-start(bf16[8,96,2048]{2,1,0:T(8,128)(2,1)} %all_to_all.20), calls=%async_computation.1 | async-start | bytes 6291456 | tf_op jit(solution)/shard_map/all_to_all | solution.py:32
  294.3 97.1 %all-to-all-start.2 = ((bf16[32,768,128]{1,2,0:T(8,128)(2,1)}), bf16[32,768,128]{1,2,0:T(8,128)(2,1)}, u32[]{:S(2)}, u32[]{:S(2)}) async-start(bf16[32,768,128]{1,2,0:T(8,128)(2,1)} %broadcast_select_fusion), calls=%async_computation.2 | async-start | bytes 12582912 | tf_op jit(solution)/shard_map/all_to_all | solution.py:37
  313.4 168.3 %reduce-scatter.2.cloned.1.call-start = ((), (), s32[]{:S(2)}) async-start(), calls=%async_computation.5 | async-start | bytes 4456448 | tf_op jit(solution)/shard_map/reduce_scatter | solution.py:46
  482.7 16.0 %collective-permute-start = (bf16[8,32,2,128]{3,1,2,0:T(8,128)(2,1)S(1)}, bf16[8,32,2,128]{3,1,2,0:T(8,128)(2,1)S(1)}, u32[]{:S(2)}, u32[]{:S(2)}) collective-permute-start(bf16[8,32,2,128]{3,1,2,0:T(8,128)(2,1)S(1)} %convert_element_type.3), channel_id=1, source_target_pairs={{0,0},{1,16},{2,32},{3,48},{4,64},{5,80},{6,96},{7,112},{16,1},{17... | collective-permute-start | bytes 393224 | tf_op jit(solution)/shard_map/ppermute | solution.py:56
  499.5 26.7 %all-to-all-start.3 = ((bf16[32,2,128,8]{2,3,1,0:T(8,128)(2,1)}), bf16[32,2,128,8]{2,3,1,0:T(8,128)(2,1)S(1)}, u32[]{:S(2)}, u32[]{:S(2)}) async-start(bf16[32,2,128,8]{2,3,1,0:T(8,128)(2,1)} %copy.43), calls=%async_computation.4 | async-start | bytes 262144 | tf_op jit(solution)/shard_map/all_to_all | solution.py:61
Sparse Core Ops, SparseCore 0:
  408.0 73.7 reduce-scatter.1

commit v2 on v1

v2 whole, which is shorter than its diff:
```python
import functools

import jax
import jax.numpy as jnp
from jax import lax
from jax.experimental import pallas as pl
from jax.experimental.pallas import tpu as pltpu
from jax.sharding import Mesh, PartitionSpec as P

OBS = 4
COUPLE = 2
BS = 128
SPLIT = 3
HALVES = 2
REGION = ("x", "zlo")
RUN = ("zhi", "y", "core")
MESH = pl.DeviceIdType.MESH


def remote(src, dst, send, recv, where):
    return pltpu.make_async_remote_copy(
        src_ref=src, dst_ref=dst, send_sem=send, recv_sem=recv, device_id=where, device_id_type=MESH
    )


def loop(low, high, body):
    def step(i, carry):
        body(i)
        return carry

    lax.fori_loop(low, high, step, 0)


def gather_kernel(
    sizes, sens, counts, table, acc, masked, zbuf, outbuf, inbuf, ztab, xtab, stab,
    zs, zr, ys, yr, ps, pr, tzs, tzr, txs, txr, tsem, *tbufs,
):
    nx, nz, ny, nc = sizes
    x, zlo = lax.axis_index("x"), lax.axis_index("zlo")
    y, core = lax.axis_index("y"), lax.axis_index("core")
    rho = y * nc + core
    plane = x * nz + rho
    planes = nx * nz
    depth = tbufs[0].shape[1] * tbufs[0].shape[2]
    stride = 11 % planes
    blocks, sub = masked.shape[2], masked.shape[3]
    first_run = (lax.axis_index("zhi") * nz + rho) * (sens.shape[0] // OBS)

    def z_at(d):
        return {"zlo": lax.rem(zlo + d, nz)}

    def yc_at(t):
        return {"y": t // nc, "core": lax.rem(t, nc)}

    def x_at(d):
        return {"x": lax.rem(x + d, nx)}

    def plane_at(t):
        r = lax.rem(t, nz)
        return {"x": t // nz, "y": r // nc, "core": lax.rem(r, nc)}

    barrier = pltpu.get_barrier_semaphore()
    loop(1, nz, lambda d: pl.semaphore_signal(barrier, inc=1, device_id=z_at(d), device_id_type=MESH))
    loop(1, planes, lambda g: pl.semaphore_signal(
        barrier, inc=1, device_id=plane_at(lax.rem(plane + g, planes)), device_id_type=MESH))
    pl.semaphore_wait(barrier, nz - 1 + planes - 1)

    def table_copy(d):
        return remote(table, ztab.at[zlo], tzs.at[d], tzr.at[d], z_at(d))

    def row_copy(x_from, d):
        return remote(ztab, xtab.at[x_from], txs.at[d], txr.at[d], x_at(d))

    def z_copy(s, d):
        return remote(
            masked.at[lax.rem(zlo + d, nz), s], zbuf.at[s, zlo], zs.at[s, d], zr.at[s, d], z_at(d))

    def y_copy(s, e):
        t = lax.rem(rho + e, nz)
        return remote(zbuf.at[s, t], tbufs[s].at[:, rho], ys.at[s, e], yr.at[s, e], yc_at(t))

    def p_copy(s, g):
        return remote(
            outbuf.at[s, g], inbuf.at[s, plane], ps.at[s, g], pr.at[s, g],
            plane_at(lax.rem(plane + g, planes)))

    def mask(j, s):
        start = pl.multiple_of((j * SPLIT + s) * sub, sub)
        run = (start + lax.broadcasted_iota(jnp.int32, (sub, BS), 0)) // OBS + first_run
        for b in range(blocks):
            value = sens[pl.ds(start, sub), b * BS:(b + 1) * BS].astype(jnp.float32)
            masked[j, s, b] = jnp.where(run < counts[b], value, 0.0).astype(jnp.bfloat16)

    def z_send(s):
        def one(d):
            mask(lax.rem(zlo + d, nz), s)
            z_copy(s, d).start()

        loop(1, nz, one)
        mask(zlo, s)
        pltpu.make_async_copy(masked.at[zlo, s], zbuf.at[s, zlo], zr.at[s, 0]).start()

    def z_wait(s, d):
        dst = zbuf.at[s, lax.rem(zlo + nz - d, nz)]
        pltpu.make_async_copy(dst, dst, zr.at[s, d]).wait()

    def relay(s):
        z_wait(s, lax.rem(zlo + nz - rho, nz))
        pltpu.make_async_copy(zbuf.at[s, rho], tbufs[s].at[:, rho], yr.at[s, 0]).start()

        def one(e):
            z_wait(s, lax.rem(zlo + 2 * nz - rho - e, nz))
            y_copy(s, e).start()

        loop(1, nz, one)

    def block(s, b):
        return tbufs[s][b].reshape(depth, BS)

    def asked(t):
        return stab[t // nz, lax.rem(t, nz), 0, plane]

    def pick(s):
        def ready(e):
            dst = tbufs[s].at[:, lax.rem(rho + nz - e, nz)]
            pltpu.make_async_copy(dst, dst, yr.at[s, e]).wait()

        loop(0, nz, ready)

        def one(i):
            g = lax.rem(i * stride, planes)
            outbuf[s, g] = block(s, asked(lax.rem(plane + g, planes)))
            p_copy(s, g).start()

        loop(1, planes, one)
        inbuf[s, plane] = block(s, asked(plane))

    def multiply(s):
        def product(q):
            near = jnp.concatenate(
                [block(s, stab[x, rho, 1 + c, q]) for c in range(COUPLE)], axis=1)
            value = lax.dot_general(
                inbuf[s, q], near, (((0,), (0,)), ((), ())), preferred_element_type=jnp.float32)
            if s == 0:
                acc[q] = value
            else:
                acc[q] += value

        def one(i):
            g = lax.rem(i * stride, planes)
            q = lax.rem(plane + planes - g, planes)
            dst = inbuf.at[s, q]
            pltpu.make_async_copy(dst, dst, pr.at[s, g]).wait()
            product(q)

        product(plane)
        loop(1, planes, one)

    pltpu.make_async_copy(table, ztab.at[zlo], tzr.at[0]).start()
    loop(1, nz, lambda d: table_copy(d).start())
    z_send(0)

    def table_wait(d):
        dst = ztab.at[lax.rem(zlo + nz - d, nz)]
        pltpu.make_async_copy(dst, dst, tzr.at[d]).wait()

    loop(0, nz, table_wait)
    pltpu.make_async_copy(ztab, xtab.at[x], txr.at[0]).start()
    loop(1, nx, lambda d: row_copy(x, d).start())

    for s in range(SPLIT):
        if s + 1 < SPLIT:
            z_send(s + 1)
        relay(s)
        if s == 0:
            def row_wait(d):
                dst = xtab.at[lax.rem(x + nx - d, nx)]
                pltpu.make_async_copy(dst, dst, txr.at[d]).wait()

            loop(0, nx, row_wait)
            fetch = pltpu.make_async_copy(xtab, stab, tsem)
            fetch.start()
            fetch.wait()
        pick(s)
        if s > 0:
            multiply(s - 1)
    multiply(SPLIT - 1)

    loop(1, nz, lambda d: table_copy(d).wait_send())
    loop(1, nx, lambda d: row_copy(x, d).wait_send())
    for s in range(SPLIT):
        loop(1, nz, lambda d: z_copy(s, d).wait_send())
        loop(1, nz, lambda e: y_copy(s, e).wait_send())
        loop(1, planes, lambda g: p_copy(s, g).wait_send())


def reduce_kernel(sizes, acc, fbuf, mbuf, ring, fin, rs, rr, fs, fr, ms, mr):
    nx, nz, nh, ny, nc = sizes
    x, zlo, zhi = lax.axis_index("x"), lax.axis_index("zlo"), lax.axis_index("zhi")
    y, core = lax.axis_index("y"), lax.axis_index("core")
    rho = y * nc + core
    plane = x * nz + rho
    region = x * nz + zlo
    planes = nx * nz
    runs = nh * ny * nc
    mine = zhi * nz + rho
    depth = nh * nz
    z = zhi * nz + zlo
    part = acc.shape[1] // HALVES

    def z_of(k):
        return {"zhi": k // nz, "zlo": lax.rem(k, nz)}

    def run_of(t):
        r = lax.rem(t, nz)
        return {"zhi": t // nz, "y": r // nc, "core": lax.rem(r, nc)}

    def next_to(way):
        return z_of(lax.rem(z + (1 if way == 0 else depth - 1), depth))

    def fisher_to(t):
        return {"x": x, "zlo": rho, **run_of(t)}

    def mirror_to(e, t):
        q = 2 * z + e
        return {"x": q // nz, "zlo": lax.rem(q, nz), **run_of(t)}

    def fisher_from(k):
        return {"x": x, "y": zlo // nc, "core": lax.rem(zlo, nc), **z_of(k)}

    def mirror_from(s):
        r = lax.rem(s, nz)
        return {"x": s // nz, "y": r // nc, "core": lax.rem(r, nc), **z_of(region // 2)}

    fisher_self = zlo == rho
    mirror_self = z == region // 2

    barrier = pltpu.get_barrier_semaphore()

    def greet(where):
        pl.semaphore_signal(barrier, inc=1, device_id=where, device_id_type=MESH)

    greet(next_to(0))
    greet(next_to(1))

    def greet_fisher(k):
        @pl.when(jnp.logical_not(fisher_self & (k == z)))
        def _():
            greet(fisher_from(k))

    def greet_mirror(s):
        @pl.when(jnp.logical_not(mirror_self & (s == plane)))
        def _():
            greet(mirror_from(s))

    loop(0, depth, greet_fisher)
    loop(0, planes, greet_mirror)
    pl.semaphore_wait(
        barrier,
        2 + runs + 2 * runs - fisher_self.astype(jnp.int32) - mirror_self.astype(jnp.int32))

    def rows(h):
        return pl.ds(h * part, part)

    def chunk(way, i):
        if way == 0:
            return lax.rem(z + 2 * depth - 2 - i, depth)
        return lax.rem(z + 2 + i, depth)

    def hop(way, i, h, src):
        return remote(
            src, ring.at[way, i, rows(h)], rs.at[way, i, h], rr.at[way, i, h], next_to(way))

    def first(way, h):
        return hop(way, 0, h, acc.at[2 * chunk(way, -1) + way, rows(h)])

    def later(way, i, h):
        return hop(way, i + 1, h, ring.at[way, i, rows(h)])

    def take(way, i, h):
        dst = ring.at[way, i, rows(h)]
        pltpu.make_async_copy(dst, dst, rr.at[way, i, h]).wait()
        ring[way, i, rows(h)] += acc[2 * chunk(way, i) + way, rows(h)]

    for h in range(HALVES):
        for way in range(2):
            first(way, h).start()

    def step(i):
        for h in range(HALVES):
            for way in range(2):
                take(way, i, h)
                later(way, i, h).start()

    loop(0, depth - 2, step)
    for way in range(2):
        for h in range(HALVES):
            take(way, depth - 2, h)
        total = ring[way, depth - 2].T
        slices = total.reshape(COUPLE, runs, BS // runs, BS)
        for c in range(COUPLE):
            fin[:, way, c] = slices[c]

    def out_f(t):
        return remote(fin.at[t], fbuf.at[pl.ds(2 * z, 2)], fs.at[t], fr.at[z], fisher_to(t))

    def out_m(e, t):
        return remote(fin.at[t, e], mbuf.at[plane], ms.at[e, t], mr.at[plane], mirror_to(e, t))

    def self_f():
        return pltpu.make_async_copy(fin.at[mine], fbuf.at[pl.ds(2 * z, 2)], fr.at[z])

    def self_m():
        return pltpu.make_async_copy(
            fin.at[mine, lax.rem(region, 2)], mbuf.at[plane], mr.at[plane])

    def is_self_m(e, t):
        return (2 * z + e == region) & (t == mine)

    def send(k):
        t = lax.rem(mine + k, runs)

        @pl.when(jnp.logical_not(fisher_self & (t == mine)))
        def _():
            out_f(t).start()

        for e in range(2):
            @pl.when(jnp.logical_not(is_self_m(e, t)))
            def _():
                out_m(e, t).start()

    loop(0, runs, send)

    @pl.when(fisher_self)
    def _():
        self_f().start()

    @pl.when(mirror_self)
    def _():
        self_m().start()

    def got_f(k):
        dst = fbuf.at[pl.ds(2 * k, 2)]
        pltpu.make_async_copy(dst, dst, fr.at[k]).wait()

    def got_m(s):
        dst = mbuf.at[s]
        pltpu.make_async_copy(dst, dst, mr.at[s]).wait()

    loop(0, depth, got_f)
    loop(0, planes, got_m)

    for h in range(HALVES):
        for way in range(2):
            first(way, h).wait_send()

    def sent(i):
        for h in range(HALVES):
            for way in range(2):
                later(way, i, h).wait_send()

    loop(0, depth - 2, sent)

    def sent_out(t):
        @pl.when(jnp.logical_not(fisher_self & (t == mine)))
        def _():
            out_f(t).wait_send()

        for e in range(2):
            @pl.when(jnp.logical_not(is_self_m(e, t)))
            def _():
                out_m(e, t).wait_send()

    loop(0, runs, sent_out)


def shards(sensitivity, run_counts, req_owner, req_block, coupled):
    rows_dev, cols = sensitivity.shape
    blocks = run_counts.shape[0]
    nx, nz, nh, ny, nc = (lax.axis_size(a) for a in ("x", "zlo", "zhi", "y", "core"))
    regions = nx * nz
    runs = nh * ny * nc
    sub = rows_dev // (nz * SPLIT)
    vmem = pl.BlockSpec(memory_space=pltpu.VMEM)
    dma = pltpu.SemaphoreType.DMA

    fields = jnp.concatenate([req_block[:, None], coupled], axis=1)
    hit = req_owner[:, 0][:, None] == jnp.arange(regions, dtype=jnp.int32)[None, :]
    sorted_fields = jnp.sum(jnp.where(hit[:, None, :], fields[:, :, None], 0), axis=0)
    table = jnp.pad(sorted_fields, ((0, 8 - 1 - COUPLE), (0, 128 - regions)))

    acc = pl.pallas_call(
        functools.partial(gather_kernel, (nx, nz, ny, nc)),
        out_shape=jax.ShapeDtypeStruct((regions, BS, COUPLE * BS), jnp.float32),
        in_specs=[vmem, pl.BlockSpec(memory_space=pltpu.SMEM), vmem],
        out_specs=vmem,
        scratch_shapes=[
            pltpu.VMEM((nz, SPLIT, blocks, sub, BS), jnp.bfloat16),
            pltpu.VMEM((SPLIT, nz, blocks, sub, BS), jnp.bfloat16),
            pltpu.VMEM((SPLIT, regions, nz * sub, BS), jnp.bfloat16),
            pltpu.VMEM((SPLIT, regions, nz * sub, BS), jnp.bfloat16),
            pltpu.VMEM((nz, 8, 128), jnp.int32),
            pltpu.VMEM((nx, nz, 8, 128), jnp.int32),
            pltpu.SMEM((nx, nz, 8, 128), jnp.int32),
            dma((SPLIT, nz)), dma((SPLIT, nz)),
            dma((SPLIT, nz)), dma((SPLIT, nz)),
            dma((SPLIT, regions)), dma((SPLIT, regions)),
            dma((nz,)), dma((nz,)), dma((nx,)), dma((nx,)), dma,
        ] + [pltpu.VMEM((blocks, nz, sub, BS), jnp.bfloat16)] * SPLIT,
        compiler_params=pltpu.CompilerParams(
            collective_id=0, has_side_effects=True, vmem_limit_bytes=48 << 20),
    )(sensitivity, run_counts, table)

    share = BS // runs
    depth = nh * nz
    by_owner, by_source = pl.pallas_call(
        functools.partial(reduce_kernel, (nx, nz, nh, ny, nc)),
        out_shape=[jax.ShapeDtypeStruct((regions, COUPLE, share, BS), jnp.float32)] * 2,
        in_specs=[vmem],
        out_specs=[vmem, vmem],
        scratch_shapes=[
            pltpu.VMEM((2, depth - 1, BS, COUPLE * BS), jnp.float32),
            pltpu.VMEM((runs, 2, COUPLE, share, BS), jnp.float32),
            dma((2, depth - 1, HALVES)), dma((2, depth - 1, HALVES)),
            dma((runs,)), dma((depth,)),
            dma((2, runs)), dma((regions,)),
        ],
        compiler_params=pltpu.CompilerParams(
            collective_id=1, has_side_effects=True, vmem_limit_bytes=32 << 20),
    )(acc)

    fisher = jnp.take(by_owner, req_owner[:, 0], axis=0).astype(jnp.bfloat16)
    mirror = jnp.swapaxes(by_source, 2, 3).astype(jnp.bfloat16)
    return fisher, mirror.reshape(1, regions, 1, COUPLE, BS, share)


def solution(mesh):
    fine = Mesh(mesh.devices.reshape(4, 8, 2, 4, 2), ("x", "zlo", "zhi", "y", "core"))
    return build(fine)


def build(fine):
    in_specs = (P(RUN, REGION), P(REGION), P(REGION, None), P(REGION), P(REGION, None))
    out_specs = (P(REGION, None, RUN, None), P(REGION, None, None, None, None, RUN))
    return jax.shard_map(shards, mesh=fine, in_specs=in_specs, out_specs=out_specs, check_vma=False)
```

time: 542 us -> 361 us (0.67); the launches traced: 534 us -> 361 us
  Pallas kernels: 0 us -> 352 us
  blocking collectives: 256 us -> 0 us
  waiting for transfers between devices: 157 us -> 0 us
  starting transfers between devices: 53.6 us -> 0 us
  local copies, waits for them, and re-layouts: 30.5 us -> 5.34 us
  between operations: 14.3 us -> 0.7 us
  matrix products: 10.9 us -> 0 us
  other arithmetic: 11.3 us -> 2.97 us
    pallas_call x0 -> x2, Pallas kernels: none -> 352 us  [the longest x1 202 us: shards(): pl.pallas_call(functools.partial(gather_kernel, (nx, nz, ny, nc)), out_sh...]
    all_to_all x1 -> x0, blocking collectives: 153 us -> none  [shards(): lax.all_to_all(masked.reshape(zlo, chunk, blocks * BS), 'zlo', 0, 0, tile...]
    all_gather x1 -> x0, blocking collectives: 103 us -> none  [shards(): tables = lax.all_gather(table, REGION, axis=0, tiled=False)]
    all_to_all x3 -> x0, waiting for transfers between devices: 80.5 us -> none  [the longest x1 70.1 us: shards(): arrived = lax.all_to_all(outgoing, PLANE, 0, 0, tiled=True)]
    reduce_scatter x1 -> x0, waiting for transfers between devices: 73.9 us -> none  [shards(): lax.psum_scatter(partial_value, ('zhi', 'zlo'), scatter_dimension=0, tile...]
    all_to_all x3 -> x0, starting transfers between devices: 40.2 us -> none  [the longest x1 19.1 us: shards(): arrived = lax.all_to_all(outgoing, PLANE, 0, 0, tiled=True)]
    gather x4 -> x1, local copies, waits for them, and re-layouts: 20.6 us -> 0.6 us  [shards(): fisher = jnp.take(by_owner, req_owner[:, 0], axis=0).astype(jnp.bfloat16)]
    ppermute x1 -> x0, starting transfers between devices: 13.3 us -> none  [shards(): slices = lax.ppermute(held, ('zlo', 'y', 'core'), pairs)]
  transfers between devices with their start and end apart: 5 -> 0, of which waited for: 4 -> 0; matrix products, arithmetic and copies ran while one was open for 2% -> 0% of each run, Pallas kernels for 0% -> 0%
where the time goes in v2:
time: 361 us
  Pallas kernels  352 us (98%)
  local copies, waits for them, and re-layouts  5.34 us (1%)
    pallas_call x1, Pallas kernels, shards(): pl.pallas_call(functools.partial(gather_kernel, (nx, nz, ny, nc)), out_sh...  202 us
    pallas_call x1, Pallas kernels, shards(): pl.pallas_call(functools.partial(reduce_kernel, (nx, nz, nh, ny, nc)), ou...  150 us

profile of v2, /device:TPU:1, one launch (start us, length us, event | category | flops | bytes accessed | tf_op | source)
XLA Modules:
  0.0 361.2 jit_solution(8454403986434577820)
XLA Ops:
  0.6 0.7 iota_compare_fusion
  1.4 0.7 pad_add_fusion
  2.0 0.1 select_reduce_fusion
  2.2 0.0 copy-start.1
  2.2 1.9 copy-done.1
  4.0 0.0 copy-start.2
  4.1 0.7 copy-done.2
  4.7 0.0 copy-start.3
  4.7 201.7 %shard_map.68.acc = f32[32,128,256]{2,1,0:T(8,128)} custom-call(bf16[768,2048]{1,0:T(8,128)(2,1)S(1)} %copy-done.1, s32[16]{0:T(128)S(1)} %copy-done.2, s32[8,128]{1,0:T(8,128)S(1)} %pad.4.table), custom_call_target="tpu_custom_call" | custom-call | tf_op jit(solution)/shard_map/pallas_call | solution.py:392
  206.4 0.0 copy-start
  206.4 2.2 copy-done
  208.6 150.5 %shard_map.69 = (f32[32,2,8,128]{3,2,1,0:T(8,128)S(1)}, f32[32,2,8,128]{3,2,1,0:T(8,128)S(1)}) custom-call(f32[32,128,256]{2,1,0:T(8,128)S(1)} %copy-done), custom_call_target="tpu_custom_call" | custom-call | tf_op jit(solution)/shard_map/pallas_call | solution.py:416
  359.1 0.0 copy-done.3
  359.1 0.6 gather_fusion
  359.8 0.8 select_convert_fusion
  360.5 0.7 convert_bitcast_fusion
  (4 shorter events, 0.0 us)
Async XLA Ops:
  2.2 1.9 copy-start.1
  4.0 0.7 copy-start.2
  4.7 354.4 %copy-start.3 = (s32[32,1]{0,1:T(1,128)S(1)}, s32[32,1]{0,1:T(1,128)}, u32[]{:S(2)}) copy-start(s32[32,1]{0,1:T(1,128)} %param.7) | copy-start | bytes 388
  206.4 2.2 copy-start

commit v3 on v2

--- a/solution.py
+++ b/solution.py
@@ -10,8 +10,9 @@
 OBS = 4
 COUPLE = 2
 BS = 128
-SPLIT = 3
-HALVES = 2
+PARTS = (2, 2, 1, 1)
+SPLIT = len(PARTS)
+PIECES = 4
 REGION = ("x", "zlo")
 RUN = ("zhi", "y", "core")
 MESH = pl.DeviceIdType.MESH
@@ -32,18 +33,21 @@
 
 
 def gather_kernel(
-    sizes, sens, counts, table, acc, masked, zbuf, outbuf, inbuf, ztab, xtab, stab,
-    zs, zr, ys, yr, ps, pr, tzs, tzr, txs, txr, tsem, *tbufs,
+    sizes, sens, counts, table, acc, ztab, xtab, stab,
+    zs, zr, ys, yr, ps, pr, tzs, tzr, txs, txr, tsem, *bufs,
 ):
+    masked, zbufs, tbufs, outbufs, inbufs = (
+        bufs[i * SPLIT:(i + 1) * SPLIT] for i in range(5))
     nx, nz, ny, nc = sizes
     x, zlo = lax.axis_index("x"), lax.axis_index("zlo")
     y, core = lax.axis_index("y"), lax.axis_index("core")
     rho = y * nc + core
     plane = x * nz + rho
     planes = nx * nz
-    depth = tbufs[0].shape[1] * tbufs[0].shape[2]
     stride = 11 % planes
-    blocks, sub = masked.shape[2], masked.shape[3]
+    blocks = masked[0].shape[1]
+    sub = [m.shape[2] for m in masked]
+    offset = [sum(sub[:s]) for s in range(SPLIT)]
     first_run = (lax.axis_index("zhi") * nz + rho) * (sens.shape[0] // OBS)
 
     def z_at(d):
@@ -63,7 +67,6 @@
     loop(1, nz, lambda d: pl.semaphore_signal(barrier, inc=1, device_id=z_at(d), device_id_type=MESH))
     loop(1, planes, lambda g: pl.semaphore_signal(
         barrier, inc=1, device_id=plane_at(lax.rem(plane + g, planes)), device_id_type=MESH))
-    pl.semaphore_wait(barrier, nz - 1 + planes - 1)
 
     def table_copy(d):
         return remote(table, ztab.at[zlo], tzs.at[d], tzr.at[d], z_at(d))
@@ -73,40 +76,42 @@
 
     def z_copy(s, d):
         return remote(
-            masked.at[lax.rem(zlo + d, nz), s], zbuf.at[s, zlo], zs.at[s, d], zr.at[s, d], z_at(d))
+            masked[s].at[lax.rem(zlo + d, nz)], zbufs[s].at[zlo], zs.at[s, d], zr.at[s, d], z_at(d))
 
     def y_copy(s, e):
         t = lax.rem(rho + e, nz)
-        return remote(zbuf.at[s, t], tbufs[s].at[:, rho], ys.at[s, e], yr.at[s, e], yc_at(t))
+        return remote(zbufs[s].at[t], tbufs[s].at[:, rho], ys.at[s, e], yr.at[s, e], yc_at(t))
 
     def p_copy(s, g):
         return remote(
-            outbuf.at[s, g], inbuf.at[s, plane], ps.at[s, g], pr.at[s, g],
+            outbufs[s].at[g], inbufs[s].at[plane], ps.at[s, g], pr.at[s, g],
             plane_at(lax.rem(plane + g, planes)))
 
     def mask(j, s):
-        start = pl.multiple_of((j * SPLIT + s) * sub, sub)
-        run = (start + lax.broadcasted_iota(jnp.int32, (sub, BS), 0)) // OBS + first_run
+        start = pl.multiple_of(j * sum(sub) + offset[s], sub[-1])
+        run = (start + lax.broadcasted_iota(jnp.int32, (sub[s], BS), 0)) // OBS + first_run
         for b in range(blocks):
-            value = sens[pl.ds(start, sub), b * BS:(b + 1) * BS].astype(jnp.float32)
-            masked[j, s, b] = jnp.where(run < counts[b], value, 0.0).astype(jnp.bfloat16)
+            value = sens[pl.ds(start, sub[s]), b * BS:(b + 1) * BS].astype(jnp.float32)
+            masked[s][j, b] = jnp.where(run < counts[b], value, 0.0).astype(jnp.bfloat16)
 
     def z_send(s):
         def one(d):
-            mask(lax.rem(zlo + d, nz), s)
+            if s > 0:
+                mask(lax.rem(zlo + d, nz), s)
             z_copy(s, d).start()
 
         loop(1, nz, one)
-        mask(zlo, s)
-        pltpu.make_async_copy(masked.at[zlo, s], zbuf.at[s, zlo], zr.at[s, 0]).start()
+        if s > 0:
+            mask(zlo, s)
+        pltpu.make_async_copy(masked[s].at[zlo], zbufs[s].at[zlo], zr.at[s, 0]).start()
 
     def z_wait(s, d):
-        dst = zbuf.at[s, lax.rem(zlo + nz - d, nz)]
+        dst = zbufs[s].at[lax.rem(zlo + nz - d, nz)]
         pltpu.make_async_copy(dst, dst, zr.at[s, d]).wait()
 
     def relay(s):
         z_wait(s, lax.rem(zlo + nz - rho, nz))
-        pltpu.make_async_copy(zbuf.at[s, rho], tbufs[s].at[:, rho], yr.at[s, 0]).start()
+        pltpu.make_async_copy(zbufs[s].at[rho], tbufs[s].at[:, rho], yr.at[s, 0]).start()
 
         def one(e):
             z_wait(s, lax.rem(zlo + 2 * nz - rho - e, nz))
@@ -115,7 +120,7 @@
         loop(1, nz, one)
 
     def block(s, b):
-        return tbufs[s][b].reshape(depth, BS)
+        return tbufs[s][b].reshape(nz * sub[s], BS)
 
     def asked(t):
         return stab[t // nz, lax.rem(t, nz), 0, plane]
@@ -129,18 +134,18 @@
 
         def one(i):
             g = lax.rem(i * stride, planes)
-            outbuf[s, g] = block(s, asked(lax.rem(plane + g, planes)))
+            outbufs[s][g] = block(s, asked(lax.rem(plane + g, planes)))
             p_copy(s, g).start()
 
         loop(1, planes, one)
-        inbuf[s, plane] = block(s, asked(plane))
+        inbufs[s][plane] = block(s, asked(plane))
 
     def multiply(s):
         def product(q):
             near = jnp.concatenate(
                 [block(s, stab[x, rho, 1 + c, q]) for c in range(COUPLE)], axis=1)
             value = lax.dot_general(
-                inbuf[s, q], near, (((0,), (0,)), ((), ())), preferred_element_type=jnp.float32)
+                inbufs[s][q], near, (((0,), (0,)), ((), ())), preferred_element_type=jnp.float32)
             if s == 0:
                 acc[q] = value
             else:
@@ -149,12 +154,15 @@
         def one(i):
             g = lax.rem(i * stride, planes)
             q = lax.rem(plane + planes - g, planes)
-            dst = inbuf.at[s, q]
+            dst = inbufs[s].at[q]
             pltpu.make_async_copy(dst, dst, pr.at[s, g]).wait()
             product(q)
 
         product(plane)
         loop(1, planes, one)
+
+    loop(0, nz, lambda j: mask(j, 0))
+    pl.semaphore_wait(barrier, nz - 1 + planes - 1)
 
     pltpu.make_async_copy(table, ztab.at[zlo], tzr.at[0]).start()
     loop(1, nz, lambda d: table_copy(d).start())
@@ -206,7 +214,7 @@
     mine = zhi * nz + rho
     depth = nh * nz
     z = zhi * nz + zlo
-    part = acc.shape[1] // HALVES
+    part = acc.shape[1] // PIECES
 
     def z_of(k):
         return {"zhi": k // nz, "zlo": lax.rem(k, nz)}
@@ -282,24 +290,23 @@
         pltpu.make_async_copy(dst, dst, rr.at[way, i, h]).wait()
         ring[way, i, rows(h)] += acc[2 * chunk(way, i) + way, rows(h)]
 
-    for h in range(HALVES):
+    for h in range(PIECES):
         for way in range(2):
             first(way, h).start()
 
     def step(i):
-        for h in range(HALVES):
+        for h in range(PIECES):
             for way in range(2):
                 take(way, i, h)
                 later(way, i, h).start()
 
     loop(0, depth - 2, step)
     for way in range(2):
-        for h in range(HALVES):
+        for h in range(PIECES):
             take(way, depth - 2, h)
         total = ring[way, depth - 2].T
         slices = total.reshape(COUPLE, runs, BS // runs, BS)
-        for c in range(COUPLE):
-            fin[:, way, c] = slices[c]
+        fin[:, way] = jnp.concatenate([slices[c] for c in range(COUPLE)], axis=1).astype(jnp.bfloat16)
 
     def out_f(t):
         return remote(fin.at[t], fbuf.at[pl.ds(2 * z, 2)], fs.at[t], fr.at[z], fisher_to(t))
@@ -350,12 +357,12 @@
     loop(0, depth, got_f)
     loop(0, planes, got_m)
 
-    for h in range(HALVES):
+    for h in range(PIECES):
         for way in range(2):
             first(way, h).wait_send()
 
     def sent(i):
-        for h in range(HALVES):
+        for h in range(PIECES):
             for way in range(2):
                 later(way, i, h).wait_send()
 
@@ -380,7 +387,7 @@
     nx, nz, nh, ny, nc = (lax.axis_size(a) for a in ("x", "zlo", "zhi", "y", "core"))
     regions = nx * nz
     runs = nh * ny * nc
-    sub = rows_dev // (nz * SPLIT)
+    sub = [n * rows_dev // (nz * sum(PARTS)) for n in PARTS]
     vmem = pl.BlockSpec(memory_space=pltpu.VMEM)
     dma = pltpu.SemaphoreType.DMA
 
@@ -395,10 +402,6 @@
         in_specs=[vmem, pl.BlockSpec(memory_space=pltpu.SMEM), vmem],
         out_specs=vmem,
         scratch_shapes=[
-            pltpu.VMEM((nz, SPLIT, blocks, sub, BS), jnp.bfloat16),
-            pltpu.VMEM((SPLIT, nz, blocks, sub, BS), jnp.bfloat16),
-            pltpu.VMEM((SPLIT, regions, nz * sub, BS), jnp.bfloat16),
-            pltpu.VMEM((SPLIT, regions, nz * sub, BS), jnp.bfloat16),
             pltpu.VMEM((nz, 8, 128), jnp.int32),
             pltpu.VMEM((nx, nz, 8, 128), jnp.int32),
             pltpu.SMEM((nx, nz, 8, 128), jnp.int32),
@@ -406,7 +409,13 @@
             dma((SPLIT, nz)), dma((SPLIT, nz)),
             dma((SPLIT, regions)), dma((SPLIT, regions)),
             dma((nz,)), dma((nz,)), dma((nx,)), dma((nx,)), dma,
-        ] + [pltpu.VMEM((blocks, nz, sub, BS), jnp.bfloat16)] * SPLIT,
+        ] + [
+            pltpu.VMEM(shape, jnp.bfloat16)
+            for shape in (
+                [(nz, blocks, n, BS) for n in sub] * 2
+                + [(blocks, nz, n, BS) for n in sub]
+                + [(regions, nz * n, BS) for n in sub] * 2)
+        ],
         compiler_params=pltpu.CompilerParams(
             collective_id=0, has_side_effects=True, vmem_limit_bytes=48 << 20),
     )(sensitivity, run_counts, table)
@@ -415,13 +424,13 @@
     depth = nh * nz
     by_owner, by_source = pl.pallas_call(
         functools.partial(reduce_kernel, (nx, nz, nh, ny, nc)),
-        out_shape=[jax.ShapeDtypeStruct((regions, COUPLE, share, BS), jnp.float32)] * 2,
+        out_shape=[jax.ShapeDtypeStruct((regions, COUPLE * share, BS), jnp.bfloat16)] * 2,
         in_specs=[vmem],
         out_specs=[vmem, vmem],
         scratch_shapes=[
             pltpu.VMEM((2, depth - 1, BS, COUPLE * BS), jnp.float32),
-            pltpu.VMEM((runs, 2, COUPLE, share, BS), jnp.float32),
-            dma((2, depth - 1, HALVES)), dma((2, depth - 1, HALVES)),
+            pltpu.VMEM((runs, 2, COUPLE * share, BS), jnp.bfloat16),
+            dma((2, depth - 1, PIECES)), dma((2, depth - 1, PIECES)),
             dma((runs,)), dma((depth,)),
             dma((2, runs)), dma((regions,)),
         ],
@@ -429,8 +438,8 @@
             collective_id=1, has_side_effects=True, vmem_limit_bytes=32 << 20),
     )(acc)
 
-    fisher = jnp.take(by_owner, req_owner[:, 0], axis=0).astype(jnp.bfloat16)
-    mirror = jnp.swapaxes(by_source, 2, 3).astype(jnp.bfloat16)
+    fisher = jnp.take(by_owner, req_owner[:, 0], axis=0).reshape(-1, COUPLE, share, BS)
+    mirror = jnp.swapaxes(by_source.reshape(-1, COUPLE, share, BS), 2, 3)
     return fisher, mirror.reshape(1, regions, 1, COUPLE, BS, share)
 
 

time: 361 us -> 348 us (0.964); the launches traced: 361 us -> 343 us
  Pallas kernels: 352 us -> 334 us
    pallas_call x1, Pallas kernels: 150 us -> 127 us  [shards(): pl.pallas_call(functools.partial(reduce_kernel, (nx, nz, nh, ny, nc)), ou...]
    pallas_call x1, Pallas kernels: 202 us -> 208 us  [shards(): pl.pallas_call(functools.partial(gather_kernel, (nx, nz, ny, nc)), out_sh...]
where the time goes in v3:
time: 348 us; the launch traced here: 343 us
  Pallas kernels  334 us (96%)
  local copies, waits for them, and re-layouts  5.98 us (2%)
    pallas_call x1, Pallas kernels, shards(): pl.pallas_call(functools.partial(gather_kernel, (nx, nz, ny, nc)), out_sh...  208 us
    pallas_call x1, Pallas kernels, shards(): pl.pallas_call(functools.partial(reduce_kernel, (nx, nz, nh, ny, nc)), ou...  127 us

profile of v3, /device:TPU:1, one launch (start us, length us, event | category | flops | bytes accessed | tf_op | source)
XLA Modules:
  0.0 343.3 jit_solution(7899737789154054428)
XLA Ops:
  0.6 0.7 iota_compare_fusion
  1.4 0.7 pad_add_fusion
  2.0 0.1 select_reduce_fusion
  2.2 0.0 copy-start.1
  2.2 1.9 copy-done.1
  4.0 0.0 copy-start.2
  4.1 0.7 copy-done.2
  4.7 0.0 copy-start.3
  4.7 207.6 %shard_map.68.acc = f32[32,128,256]{2,1,0:T(8,128)} custom-call(bf16[768,2048]{1,0:T(8,128)(2,1)S(1)} %copy-done.1, s32[16]{0:T(128)S(1)} %copy-done.2, s32[8,128]{1,0:T(8,128)S(1)} %pad.4.table), custom_call_target="tpu_custom_call" | custom-call | tf_op jit(solution)/shard_map/pallas_call | solution.py:399
  212.3 0.0 copy-start
  212.3 2.2 copy-done
  214.5 126.8 %shard_map.69 = (bf16[32,16,128]{2,1,0:T(8,128)(2,1)S(1)}, bf16[32,16,128]{2,1,0:T(8,128)(2,1)S(1)}) custom-call(f32[32,128,256]{2,1,0:T(8,128)S(1)} %copy-done), custom_call_target="tpu_custom_call" | custom-call | tf_op jit(solution)/shard_map/pallas_call | solution.py:425
  341.3 0.0 copy-done.3
  341.3 0.6 gather_fusion
  341.9 0.8 bitcast_select_fusion
  342.7 0.7 copy.9
  (4 shorter events, 0.0 us)
Async XLA Ops:
  2.2 1.9 copy-start.1
  4.0 0.7 copy-start.2
  4.7 336.6 %copy-start.3 = (s32[32,1]{0,1:T(1,128)S(1)}, s32[32,1]{0,1:T(1,128)}, u32[]{:S(2)}) copy-start(s32[32,1]{0,1:T(1,128)} %param.7) | copy-start | bytes 388
  212.3 2.2 copy-start

commit v4 on v3

--- a/solution.py
+++ b/solution.py
@@ -36,8 +36,8 @@
     sizes, sens, counts, table, acc, ztab, xtab, stab,
     zs, zr, ys, yr, ps, pr, tzs, tzr, txs, txr, tsem, *bufs,
 ):
-    masked, zbufs, tbufs, outbufs, inbufs = (
-        bufs[i * SPLIT:(i + 1) * SPLIT] for i in range(5))
+    masked, zbufs, tbufs, turned, outbufs, inbufs = (
+        bufs[i * SPLIT:(i + 1) * SPLIT] for i in range(6))
     nx, nz, ny, nc = sizes
     x, zlo = lax.axis_index("x"), lax.axis_index("zlo")
     y, core = lax.axis_index("y"), lax.axis_index("core")
@@ -95,7 +95,8 @@
             masked[s][j, b] = jnp.where(run < counts[b], value, 0.0).astype(jnp.bfloat16)
 
     def z_send(s):
-        def one(d):
+        def one(i):
+            d = lax.rem(i * 3, nz)
             if s > 0:
                 mask(lax.rem(zlo + d, nz), s)
             z_copy(s, d).start()
@@ -110,14 +111,20 @@
         pltpu.make_async_copy(dst, dst, zr.at[s, d]).wait()
 
     def relay(s):
-        z_wait(s, lax.rem(zlo + nz - rho, nz))
-        pltpu.make_async_copy(zbufs[s].at[rho], tbufs[s].at[:, rho], yr.at[s, 0]).start()
-
-        def one(e):
-            z_wait(s, lax.rem(zlo + 2 * nz - rho - e, nz))
-            y_copy(s, e).start()
-
-        loop(1, nz, one)
+        def one(i):
+            d = lax.rem(i * 3, nz)
+            z_wait(s, d)
+            e = lax.rem(zlo + 2 * nz - d - rho, nz)
+
+            @pl.when(e == 0)
+            def _():
+                pltpu.make_async_copy(zbufs[s].at[rho], tbufs[s].at[:, rho], yr.at[s, 0]).start()
+
+            @pl.when(e > 0)
+            def _():
+                y_copy(s, e).start()
+
+        loop(0, nz, one)
 
     def block(s, b):
         return tbufs[s][b].reshape(nz * sub[s], BS)
@@ -140,12 +147,17 @@
         loop(1, planes, one)
         inbufs[s][plane] = block(s, asked(plane))
 
+    def turn(s):
+        def one(b):
+            turned[s][b] = tbufs[s][b].reshape(nz * sub[s], BS).T
+
+        loop(0, blocks, one)
+
     def multiply(s):
         def product(q):
             near = jnp.concatenate(
-                [block(s, stab[x, rho, 1 + c, q]) for c in range(COUPLE)], axis=1)
-            value = lax.dot_general(
-                inbufs[s][q], near, (((0,), (0,)), ((), ())), preferred_element_type=jnp.float32)
+                [turned[s][stab[x, rho, 1 + c, q]] for c in range(COUPLE)], axis=0)
+            value = jnp.dot(near, inbufs[s][q], preferred_element_type=jnp.float32)
             if s == 0:
                 acc[q] = value
             else:
@@ -172,14 +184,17 @@
         dst = ztab.at[lax.rem(zlo + nz - d, nz)]
         pltpu.make_async_copy(dst, dst, tzr.at[d]).wait()
 
+    z_send(1)
     loop(0, nz, table_wait)
     pltpu.make_async_copy(ztab, xtab.at[x], txr.at[0]).start()
     loop(1, nx, lambda d: row_copy(x, d).start())
 
     for s in range(SPLIT):
-        if s + 1 < SPLIT:
-            z_send(s + 1)
+        if s + 2 < SPLIT:
+            z_send(s + 2)
         relay(s)
+        if s > 0:
+            multiply(s - 1)
         if s == 0:
             def row_wait(d):
                 dst = xtab.at[lax.rem(x + nx - d, nx)]
@@ -190,8 +205,7 @@
             fetch.start()
             fetch.wait()
         pick(s)
-        if s > 0:
-            multiply(s - 1)
+        turn(s)
     multiply(SPLIT - 1)
 
     loop(1, nz, lambda d: table_copy(d).wait_send())
@@ -214,7 +228,9 @@
     mine = zhi * nz + rho
     depth = nh * nz
     z = zhi * nz + zlo
-    part = acc.shape[1] // PIECES
+    ahead = [depth // 2, depth - 1 - depth // 2]
+    pieces = [(e, h) for h in range(PIECES // 2) for e in range(2)]
+    part = acc.shape[1] // (PIECES // 2)
 
     def z_of(k):
         return {"zhi": k // nz, "zlo": lax.rem(k, nz)}
@@ -272,41 +288,52 @@
 
     def chunk(way, i):
         if way == 0:
-            return lax.rem(z + 2 * depth - 2 - i, depth)
-        return lax.rem(z + 2 + i, depth)
-
-    def hop(way, i, h, src):
+            return lax.rem(z + depth - 1 + ahead[0] - i, depth)
+        return lax.rem(z + depth + 1 - ahead[1] + i, depth)
+
+    def hop(way, i, p, src):
+        e, h = pieces[p]
         return remote(
-            src, ring.at[way, i, rows(h)], rs.at[way, i, h], rr.at[way, i, h], next_to(way))
-
-    def first(way, h):
-        return hop(way, 0, h, acc.at[2 * chunk(way, -1) + way, rows(h)])
-
-    def later(way, i, h):
-        return hop(way, i + 1, h, ring.at[way, i, rows(h)])
-
-    def take(way, i, h):
-        dst = ring.at[way, i, rows(h)]
-        pltpu.make_async_copy(dst, dst, rr.at[way, i, h]).wait()
-        ring[way, i, rows(h)] += acc[2 * chunk(way, i) + way, rows(h)]
-
-    for h in range(PIECES):
-        for way in range(2):
-            first(way, h).start()
-
-    def step(i):
-        for h in range(PIECES):
-            for way in range(2):
-                take(way, i, h)
-                later(way, i, h).start()
-
-    loop(0, depth - 2, step)
-    for way in range(2):
-        for h in range(PIECES):
-            take(way, depth - 2, h)
-        total = ring[way, depth - 2].T
+            src, ring.at[way, i, e, rows(h)], rs.at[way, i, p], rr.at[way, i, p], next_to(way))
+
+    def first(way, p):
+        e, h = pieces[p]
+        own = lax.rem(z + depth + (ahead[0] if way == 0 else -ahead[1]), depth)
+        return hop(way, 0, p, acc.at[2 * own + e, rows(h)])
+
+    def later(way, i, p):
+        e, h = pieces[p]
+        return hop(way, i + 1, p, ring.at[way, i, e, rows(h)])
+
+    def arrive(way, i, p):
+        e, h = pieces[p]
+        dst = ring.at[way, i, e, rows(h)]
+        pltpu.make_async_copy(dst, dst, rr.at[way, i, p]).wait()
+
+    def step(i, ways):
+        for p, (e, h) in enumerate(pieces):
+            for way in ways:
+                arrive(way, i, p)
+                ring[way, i, e, rows(h)] += acc[2 * chunk(way, i) + e, rows(h)]
+                later(way, i, p).start()
+
+    ways = [way for way in range(2) if ahead[way] > 0]
+    both = max(0, ahead[1] - 1)
+    for p in range(len(pieces)):
+        for way in ways:
+            first(way, p).start()
+    loop(0, both, lambda i: step(i, [0, 1]))
+    for i in range(both, ahead[0] - 1):
+        step(i, [0])
+    for way in ways:
+        for p in range(len(pieces)):
+            arrive(way, ahead[way] - 1, p)
+    for e in range(2):
+        total = acc[2 * z + e]
+        for way in ways:
+            total += ring[way, ahead[way] - 1, e]
         slices = total.reshape(COUPLE, runs, BS // runs, BS)
-        fin[:, way] = jnp.concatenate([slices[c] for c in range(COUPLE)], axis=1).astype(jnp.bfloat16)
+        fin[:, e] = jnp.concatenate([slices[c] for c in range(COUPLE)], axis=1).astype(jnp.bfloat16)
 
     def out_f(t):
         return remote(fin.at[t], fbuf.at[pl.ds(2 * z, 2)], fs.at[t], fr.at[z], fisher_to(t))
@@ -357,16 +384,16 @@
     loop(0, depth, got_f)
     loop(0, planes, got_m)
 
-    for h in range(PIECES):
-        for way in range(2):
-            first(way, h).wait_send()
-
-    def sent(i):
-        for h in range(PIECES):
-            for way in range(2):
-                later(way, i, h).wait_send()
-
-    loop(0, depth - 2, sent)
+    for p in range(len(pieces)):
+        for way in ways:
+            first(way, p).wait_send()
+
+    def sent(way, i):
+        for p in range(len(pieces)):
+            later(way, i, p).wait_send()
+
+    for way in ways:
+        loop(0, ahead[way] - 1, functools.partial(sent, way))
 
     def sent_out(t):
         @pl.when(jnp.logical_not(fisher_self & (t == mine)))
@@ -398,7 +425,7 @@
 
     acc = pl.pallas_call(
         functools.partial(gather_kernel, (nx, nz, ny, nc)),
-        out_shape=jax.ShapeDtypeStruct((regions, BS, COUPLE * BS), jnp.float32),
+        out_shape=jax.ShapeDtypeStruct((regions, COUPLE * BS, BS), jnp.float32),
         in_specs=[vmem, pl.BlockSpec(memory_space=pltpu.SMEM), vmem],
         out_specs=vmem,
         scratch_shapes=[
@@ -414,6 +441,7 @@
             for shape in (
                 [(nz, blocks, n, BS) for n in sub] * 2
                 + [(blocks, nz, n, BS) for n in sub]
+                + [(blocks, BS, nz * n) for n in sub]
                 + [(regions, nz * n, BS) for n in sub] * 2)
         ],
         compiler_params=pltpu.CompilerParams(
@@ -428,9 +456,9 @@
         in_specs=[vmem],
         out_specs=[vmem, vmem],
         scratch_shapes=[
-            pltpu.VMEM((2, depth - 1, BS, COUPLE * BS), jnp.float32),
+            pltpu.VMEM((2, depth // 2, 2, COUPLE * BS, BS), jnp.float32),
             pltpu.VMEM((runs, 2, COUPLE * share, BS), jnp.bfloat16),
-            dma((2, depth - 1, PIECES)), dma((2, depth - 1, PIECES)),
+            dma((2, depth // 2, PIECES)), dma((2, depth // 2, PIECES)),
             dma((runs,)), dma((depth,)),
             dma((2, runs)), dma((regions,)),
         ],

time: 348 us -> 313 us (0.90)
  Pallas kernels: 334 us -> 301 us
    pallas_call x1, Pallas kernels: 127 us -> 103 us  [shards(): pl.pallas_call(functools.partial(reduce_kernel, (nx, nz, nh, ny, nc)), ou...]
    pallas_call x1, Pallas kernels: 208 us -> 198 us  [shards(): pl.pallas_call(functools.partial(gather_kernel, (nx, nz, ny, nc)), out_sh...]
where the time goes in v4:
time: 313 us; the launch traced here: 310 us
  Pallas kernels  301 us (96%)
  local copies, waits for them, and re-layouts  5.98 us (2%)
    pallas_call x1, Pallas kernels, shards(): pl.pallas_call(functools.partial(gather_kernel, (nx, nz, ny, nc)), out_sh...  198 us
    pallas_call x1, Pallas kernels, shards(): pl.pallas_call(functools.partial(reduce_kernel, (nx, nz, nh, ny, nc)), ou...  103 us

profile of v4, /device:TPU:1, one launch (start us, length us, event | category | flops | bytes accessed | tf_op | source)
XLA Modules:
  0.0 309.9 jit_solution(13717710265888414966)
XLA Ops:
  0.6 0.7 iota_compare_fusion
  1.4 0.7 pad_add_fusion
  2.0 0.1 select_reduce_fusion
  2.2 0.0 copy-start.1
  2.2 1.9 copy-done.1
  4.0 0.0 copy-start.2
  4.1 0.7 copy-done.2
  4.7 0.0 copy-start.3
  4.7 197.8 %shard_map.68.acc = f32[32,256,128]{2,1,0:T(8,128)} custom-call(bf16[768,2048]{1,0:T(8,128)(2,1)S(1)} %copy-done.1, s32[16]{0:T(128)S(1)} %copy-done.2, s32[8,128]{1,0:T(8,128)S(1)} %pad.4.table), custom_call_target="tpu_custom_call" | custom-call | tf_op jit(solution)/shard_map/pallas_call | solution.py:426
  202.5 0.0 copy-start
  202.5 2.2 copy-done
  204.7 103.1 %shard_map.69 = (bf16[32,16,128]{2,1,0:T(8,128)(2,1)S(1)}, bf16[32,16,128]{2,1,0:T(8,128)(2,1)S(1)}) custom-call(f32[32,256,128]{2,1,0:T(8,128)S(1)} %copy-done), custom_call_target="tpu_custom_call" | custom-call | tf_op jit(solution)/shard_map/pallas_call | solution.py:453
  307.8 0.0 copy-done.3
  307.9 0.6 gather_fusion
  308.5 0.8 bitcast_select_fusion
  309.2 0.7 copy.9
  (4 shorter events, 0.0 us)
Async XLA Ops:
  2.2 1.9 copy-start.1
  4.0 0.7 copy-start.2
  4.7 303.1 %copy-start.3 = (s32[32,1]{0,1:T(1,128)S(1)}, s32[32,1]{0,1:T(1,128)}, u32[]{:S(2)}) copy-start(s32[32,1]{0,1:T(1,128)} %param.7) | copy-start | bytes 388
  202.5 2.2 copy-start

commit v5 on v4

--- a/solution.py
+++ b/solution.py
@@ -10,9 +10,9 @@
 OBS = 4
 COUPLE = 2
 BS = 128
-PARTS = (2, 2, 1, 1)
+PARTS = (1, 2, 2, 1)
 SPLIT = len(PARTS)
-PIECES = 4
+PIECES = 8
 REGION = ("x", "zlo")
 RUN = ("zhi", "y", "core")
 MESH = pl.DeviceIdType.MESH
@@ -94,17 +94,16 @@
             value = sens[pl.ds(start, sub[s]), b * BS:(b + 1) * BS].astype(jnp.float32)
             masked[s][j, b] = jnp.where(run < counts[b], value, 0.0).astype(jnp.bfloat16)
 
-    def z_send(s):
-        def one(i):
-            d = lax.rem(i * 3, nz)
-            if s > 0:
-                mask(lax.rem(zlo + d, nz), s)
-            z_copy(s, d).start()
-
-        loop(1, nz, one)
-        if s > 0:
-            mask(zlo, s)
+    early = min(nz // 2, nz - 1)
+
+    def z_self(s):
+        mask(zlo, s)
         pltpu.make_async_copy(masked[s].at[zlo], zbufs[s].at[zlo], zr.at[s, 0]).start()
+
+    def z_one(s, i):
+        d = lax.rem(i * 3, nz)
+        mask(lax.rem(zlo + d, nz), s)
+        z_copy(s, d).start()
 
     def z_wait(s, d):
         dst = zbufs[s].at[lax.rem(zlo + nz - d, nz)]
@@ -124,7 +123,16 @@
             def _():
                 y_copy(s, e).start()
 
-        loop(0, nz, one)
+        if s + 1 < SPLIT:
+            def both(i):
+                one(i)
+                z_one(s + 1, i + 1)
+
+            loop(0, early, both)
+            loop(early, nz, one)
+            z_self(s + 1)
+        else:
+            loop(0, nz, one)
 
     def block(s, b):
         return tbufs[s][b].reshape(nz * sub[s], BS)
@@ -144,7 +152,14 @@
             outbufs[s][g] = block(s, asked(lax.rem(plane + g, planes)))
             p_copy(s, g).start()
 
-        loop(1, planes, one)
+        groups = nz - 1 - early if s + 1 < SPLIT else 0
+        begin = 1
+        for j in range(groups):
+            end = 1 + (planes - 1) * (j + 1) // (groups + 1)
+            loop(begin, end, one)
+            z_one(s + 1, early + 1 + j)
+            begin = end
+        loop(begin, planes, one)
         inbufs[s][plane] = block(s, asked(plane))
 
     def turn(s):
@@ -173,25 +188,22 @@
         product(plane)
         loop(1, planes, one)
 
-    loop(0, nz, lambda j: mask(j, 0))
     pl.semaphore_wait(barrier, nz - 1 + planes - 1)
 
     pltpu.make_async_copy(table, ztab.at[zlo], tzr.at[0]).start()
     loop(1, nz, lambda d: table_copy(d).start())
-    z_send(0)
+    loop(1, nz, lambda i: z_one(0, i))
+    z_self(0)
 
     def table_wait(d):
         dst = ztab.at[lax.rem(zlo + nz - d, nz)]
         pltpu.make_async_copy(dst, dst, tzr.at[d]).wait()
 
-    z_send(1)
     loop(0, nz, table_wait)
     pltpu.make_async_copy(ztab, xtab.at[x], txr.at[0]).start()
     loop(1, nx, lambda d: row_copy(x, d).start())
 
     for s in range(SPLIT):
-        if s + 2 < SPLIT:
-            z_send(s + 2)
         relay(s)
         if s > 0:
             multiply(s - 1)

time: 313 us -> 300 us (0.958)
  Pallas kernels: 301 us -> 287 us
    pallas_call x1, Pallas kernels: 103 us -> 90 us  [shards(): pl.pallas_call(functools.partial(reduce_kernel, (nx, nz, nh, ny, nc)), ou...]
where the time goes in v5:
time: 300 us; the launch traced here: 295 us
  Pallas kernels  287 us (96%)
  local copies, waits for them, and re-layouts  5.98 us (2%)
    pallas_call x1, Pallas kernels, shards(): pl.pallas_call(functools.partial(gather_kernel, (nx, nz, ny, nc)), out_sh...  196 us
    pallas_call x1, Pallas kernels, shards(): pl.pallas_call(functools.partial(reduce_kernel, (nx, nz, nh, ny, nc)), ou...  90 us

profile of v5, /device:TPU:1, one launch (start us, length us, event | category | flops | bytes accessed | tf_op | source)
XLA Modules:
  0.0 295.5 jit_solution(12591611363781041750)
XLA Ops:
  0.6 0.7 iota_compare_fusion
  1.4 0.7 pad_add_fusion
  2.0 0.1 select_reduce_fusion
  2.2 0.0 copy-start.1
  2.2 1.9 copy-done.1
  4.0 0.0 copy-start.2
  4.1 0.7 copy-done.2
  4.7 0.0 copy-start.3
  4.7 196.5 %shard_map.68.acc = f32[32,256,128]{2,1,0:T(8,128)} custom-call(bf16[768,2048]{1,0:T(8,128)(2,1)S(1)} %copy-done.1, s32[16]{0:T(128)S(1)} %copy-done.2, s32[8,128]{1,0:T(8,128)S(1)} %pad.4.table), custom_call_target="tpu_custom_call" | custom-call | tf_op jit(solution)/shard_map/pallas_call | solution.py:438
  201.2 0.0 copy-start
  201.2 2.2 copy-done
  203.4 90.0 %shard_map.69 = (bf16[32,16,128]{2,1,0:T(8,128)(2,1)S(1)}, bf16[32,16,128]{2,1,0:T(8,128)(2,1)S(1)}) custom-call(f32[32,256,128]{2,1,0:T(8,128)S(1)} %copy-done), custom_call_target="tpu_custom_call" | custom-call | tf_op jit(solution)/shard_map/pallas_call | solution.py:465
  293.4 0.0 copy-done.3
  293.5 0.6 gather_fusion
  294.1 0.8 bitcast_select_fusion
  294.8 0.7 copy.9
  (4 shorter events, 0.0 us)
Async XLA Ops:
  2.2 1.9 copy-start.1
  4.0 0.7 copy-start.2
  4.7 288.7 %copy-start.3 = (s32[32,1]{0,1:T(1,128)S(1)}, s32[32,1]{0,1:T(1,128)}, u32[]{:S(2)}) copy-start(s32[32,1]{0,1:T(1,128)} %param.7) | copy-start | bytes 388
  201.2 2.2 copy-start

commit v6 on v5

v6 whole, which is shorter than its diff:
```python
import functools

import jax
import jax.numpy as jnp
from jax import lax
from jax.experimental import pallas as pl
from jax.experimental.pallas import tpu as pltpu
from jax.sharding import Mesh, PartitionSpec as P

OBS = 4
COUPLE = 2
BS = 128
PARTS = (2, 1, 1, 1, 1)
SPLIT = len(PARTS)
PIECES = 8
REGION = ("x", "zlo")
RUN = ("zhi", "y", "core")
MESH = pl.DeviceIdType.MESH


def remote(src, dst, send, recv, where):
    return pltpu.make_async_remote_copy(
        src_ref=src, dst_ref=dst, send_sem=send, recv_sem=recv, device_id=where, device_id_type=MESH
    )


def loop(low, high, body):
    def step(i, carry):
        body(i)
        return carry

    lax.fori_loop(low, high, step, 0)


def reduction(sizes, barrier, acc, fbuf, mbuf, ring, fin, rs, rr, fs, fr, ms, mr):
    nx, nz, nh, ny, nc = sizes
    x, zlo, zhi = lax.axis_index("x"), lax.axis_index("zlo"), lax.axis_index("zhi")
    y, core = lax.axis_index("y"), lax.axis_index("core")
    rho = y * nc + core
    plane = x * nz + rho
    region = x * nz + zlo
    planes = nx * nz
    runs = nh * ny * nc
    mine = zhi * nz + rho
    depth = nh * nz
    z = zhi * nz + zlo
    ahead = [depth // 2, depth - 1 - depth // 2]
    pieces = [(e, h) for h in range(PIECES // 2) for e in range(2)]
    part = acc.shape[1] // (PIECES // 2)

    def z_of(k):
        return {"zhi": k // nz, "zlo": lax.rem(k, nz)}

    def run_of(t):
        r = lax.rem(t, nz)
        return {"zhi": t // nz, "y": r // nc, "core": lax.rem(r, nc)}

    def next_to(way):
        return z_of(lax.rem(z + (1 if way == 0 else depth - 1), depth))

    def fisher_to(t):
        return {"x": x, "zlo": rho, **run_of(t)}

    def mirror_to(e, t):
        q = 2 * z + e
        return {"x": q // nz, "zlo": lax.rem(q, nz), **run_of(t)}

    def fisher_from(k):
        return {"x": x, "y": zlo // nc, "core": lax.rem(zlo, nc), **z_of(k)}

    def mirror_from(s):
        r = lax.rem(s, nz)
        return {"x": s // nz, "y": r // nc, "core": lax.rem(r, nc), **z_of(region // 2)}

    fisher_self = zlo == rho
    mirror_self = z == region // 2

    def greet(where):
        pl.semaphore_signal(barrier, inc=1, device_id=where, device_id_type=MESH)

    def greet_fisher(k):
        @pl.when(jnp.logical_not(fisher_self & (k == z)))
        def _():
            greet(fisher_from(k))

    def greet_mirror(s):
        @pl.when(jnp.logical_not(mirror_self & (s == plane)))
        def _():
            greet(mirror_from(s))

    def greet_all():
        greet(next_to(0))
        greet(next_to(1))
        loop(0, depth, greet_fisher)
        loop(0, planes, greet_mirror)

    greeted = 2 + runs + 2 * runs - fisher_self.astype(jnp.int32) - mirror_self.astype(jnp.int32)

    def rows(h):
        return pl.ds(h * part, part)

    def chunk(way, i):
        if way == 0:
            return lax.rem(z + depth - 1 + ahead[0] - i, depth)
        return lax.rem(z + depth + 1 - ahead[1] + i, depth)

    def hop(way, i, p, src):
        e, h = pieces[p]
        return remote(
            src, ring.at[way, i, e, rows(h)], rs.at[way, i, p], rr.at[way, i, p], next_to(way))

    def first(way, p):
        e, h = pieces[p]
        own = lax.rem(z + depth + (ahead[0] if way == 0 else -ahead[1]), depth)
        return hop(way, 0, p, acc.at[2 * own + e, rows(h)])

    def later(way, i, p):
        e, h = pieces[p]
        return hop(way, i + 1, p, ring.at[way, i, e, rows(h)])

    def arrive(way, i, p):
        e, h = pieces[p]
        dst = ring.at[way, i, e, rows(h)]
        pltpu.make_async_copy(dst, dst, rr.at[way, i, p]).wait()

    def step(i, ways):
        for p, (e, h) in enumerate(pieces):
            for way in ways:
                arrive(way, i, p)
                ring[way, i, e, rows(h)] += acc[2 * chunk(way, i) + e, rows(h)]
                later(way, i, p).start()

    ways = [way for way in range(2) if ahead[way] > 0]
    both = max(0, ahead[1] - 1)
    def run():
        for p in range(len(pieces)):
            for way in ways:
                first(way, p).start()
        loop(0, both, lambda i: step(i, [0, 1]))
        for i in range(both, ahead[0] - 1):
            step(i, [0])
        for way in ways:
            for p in range(len(pieces)):
                arrive(way, ahead[way] - 1, p)
        for e in range(2):
            total = acc[2 * z + e]
            for way in ways:
                total += ring[way, ahead[way] - 1, e]
            slices = total.reshape(COUPLE, runs, BS // runs, BS)
            fin[:, e] = jnp.concatenate([slices[c] for c in range(COUPLE)], axis=1).astype(jnp.bfloat16)

        def out_f(t):
            return remote(fin.at[t], fbuf.at[pl.ds(2 * z, 2)], fs.at[t], fr.at[z], fisher_to(t))

        def out_m(e, t):
            return remote(fin.at[t, e], mbuf.at[plane], ms.at[e, t], mr.at[plane], mirror_to(e, t))

        def self_f():
            return pltpu.make_async_copy(fin.at[mine], fbuf.at[pl.ds(2 * z, 2)], fr.at[z])

        def self_m():
            return pltpu.make_async_copy(
                fin.at[mine, lax.rem(region, 2)], mbuf.at[plane], mr.at[plane])

        def is_self_m(e, t):
            return (2 * z + e == region) & (t == mine)

        def send(k):
            t = lax.rem(mine + k, runs)

            @pl.when(jnp.logical_not(fisher_self & (t == mine)))
            def _():
                out_f(t).start()

            for e in range(2):
                @pl.when(jnp.logical_not(is_self_m(e, t)))
                def _():
                    out_m(e, t).start()

        loop(0, runs, send)

        @pl.when(fisher_self)
        def _():
            self_f().start()

        @pl.when(mirror_self)
        def _():
            self_m().start()

        def got_f(k):
            dst = fbuf.at[pl.ds(2 * k, 2)]
            pltpu.make_async_copy(dst, dst, fr.at[k]).wait()

        def got_m(s):
            dst = mbuf.at[s]
            pltpu.make_async_copy(dst, dst, mr.at[s]).wait()

        loop(0, depth, got_f)
        loop(0, planes, got_m)

        for p in range(len(pieces)):
            for way in ways:
                first(way, p).wait_send()

        def sent(way, i):
            for p in range(len(pieces)):
                later(way, i, p).wait_send()

        for way in ways:
            loop(0, ahead[way] - 1, functools.partial(sent, way))

        def sent_out(t):
            @pl.when(jnp.logical_not(fisher_self & (t == mine)))
            def _():
                out_f(t).wait_send()

            for e in range(2):
                @pl.when(jnp.logical_not(is_self_m(e, t)))
                def _():
                    out_m(e, t).wait_send()

        loop(0, runs, sent_out)

    return greet_all, greeted, run


def fisher_kernel(
    sizes, sens, counts, table, fbuf, mbuf, acc, ring, fin, rs, rr, fs, fr, ms, mr,
    ztab, xtab, stab, zs, zr, ys, yr, ps, pr, tzs, tzr, txs, txr, tsem, *bufs,
):
    masked, zbufs, tbufs, turned, outbufs, inbufs = (
        bufs[i * SPLIT:(i + 1) * SPLIT] for i in range(6))
    nx, nz, nh, ny, nc = sizes
    x, zlo = lax.axis_index("x"), lax.axis_index("zlo")
    y, core = lax.axis_index("y"), lax.axis_index("core")
    rho = y * nc + core
    plane = x * nz + rho
    planes = nx * nz
    stride = 11 % planes
    blocks = masked[0].shape[1]
    sub = [m.shape[2] for m in masked]
    offset = [sum(sub[:s]) for s in range(SPLIT)]
    first_run = (lax.axis_index("zhi") * nz + rho) * (sens.shape[0] // OBS)

    def z_at(d):
        return {"zlo": lax.rem(zlo + d, nz)}

    def yc_at(t):
        return {"y": t // nc, "core": lax.rem(t, nc)}

    def x_at(d):
        return {"x": lax.rem(x + d, nx)}

    def plane_at(t):
        r = lax.rem(t, nz)
        return {"x": t // nz, "y": r // nc, "core": lax.rem(r, nc)}

    barrier = pltpu.get_barrier_semaphore()
    greet_all, greeted, reduce_over_z = reduction(
        sizes, barrier, acc, fbuf, mbuf, ring, fin, rs, rr, fs, fr, ms, mr)
    greet_all()
    loop(1, nz, lambda d: pl.semaphore_signal(barrier, inc=1, device_id=z_at(d), device_id_type=MESH))
    loop(1, planes, lambda g: pl.semaphore_signal(
        barrier, inc=1, device_id=plane_at(lax.rem(plane + g, planes)), device_id_type=MESH))

    def table_copy(d):
        return remote(table, ztab.at[zlo], tzs.at[d], tzr.at[d], z_at(d))

    def row_copy(x_from, d):
        return remote(ztab, xtab.at[x_from], txs.at[d], txr.at[d], x_at(d))

    def z_copy(s, d):
        return remote(
            masked[s].at[lax.rem(zlo + d, nz)], zbufs[s].at[zlo], zs.at[s, d], zr.at[s, d], z_at(d))

    def y_copy(s, e):
        t = lax.rem(rho + e, nz)
        return remote(zbufs[s].at[t], tbufs[s].at[:, rho], ys.at[s, e], yr.at[s, e], yc_at(t))

    def p_copy(s, g):
        return remote(
            outbufs[s].at[g], inbufs[s].at[plane], ps.at[s, g], pr.at[s, g],
            plane_at(lax.rem(plane + g, planes)))

    def mask(j, s):
        start = pl.multiple_of(j * sum(sub) + offset[s], sub[-1])
        run = (start + lax.broadcasted_iota(jnp.int32, (sub[s], BS), 0)) // OBS + first_run
        for b in range(blocks):
            value = sens[pl.ds(start, sub[s]), b * BS:(b + 1) * BS].astype(jnp.float32)
            masked[s][j, b] = jnp.where(run < counts[b], value, 0.0).astype(jnp.bfloat16)

    early = min(nz // 2, nz - 1)

    def z_self(s):
        mask(zlo, s)
        pltpu.make_async_copy(masked[s].at[zlo], zbufs[s].at[zlo], zr.at[s, 0]).start()

    def z_one(s, i):
        d = lax.rem(i * 3, nz)
        mask(lax.rem(zlo + d, nz), s)
        z_copy(s, d).start()

    def z_wait(s, d):
        dst = zbufs[s].at[lax.rem(zlo + nz - d, nz)]
        pltpu.make_async_copy(dst, dst, zr.at[s, d]).wait()

    def relay(s):
        def one(i):
            d = lax.rem(i * 3, nz)
            z_wait(s, d)
            e = lax.rem(zlo + 2 * nz - d - rho, nz)

            @pl.when(e == 0)
            def _():
                pltpu.make_async_copy(zbufs[s].at[rho], tbufs[s].at[:, rho], yr.at[s, 0]).start()

            @pl.when(e > 0)
            def _():
                y_copy(s, e).start()

        if s + 1 < SPLIT:
            def both(i):
                one(i)
                z_one(s + 1, i + 1)

            loop(0, early, both)
            loop(early, nz, one)
            z_self(s + 1)
        else:
            loop(0, nz, one)

    def block(s, b):
        return tbufs[s][b].reshape(nz * sub[s], BS)

    def asked(t):
        return stab[t // nz, lax.rem(t, nz), 0, plane]

    def pick(s):
        def ready(e):
            dst = tbufs[s].at[:, lax.rem(rho + nz - e, nz)]
            pltpu.make_async_copy(dst, dst, yr.at[s, e]).wait()

        loop(0, nz, ready)

        def one(i):
            g = lax.rem(i * stride, planes)
            outbufs[s][g] = block(s, asked(lax.rem(plane + g, planes)))
            p_copy(s, g).start()

        groups = nz - 1 - early if s + 1 < SPLIT else 0
        begin = 1
        for j in range(groups):
            end = 1 + (planes - 1) * (j + 1) // (groups + 1)
            loop(begin, end, one)
            z_one(s + 1, early + 1 + j)
            begin = end
        loop(begin, planes, one)
        inbufs[s][plane] = block(s, asked(plane))

    def turn(s):
        def one(b):
            turned[s][b] = tbufs[s][b].reshape(nz * sub[s], BS).T

        loop(0, blocks, one)

    def multiply(s):
        def product(q):
            near = jnp.concatenate(
                [turned[s][stab[x, rho, 1 + c, q]] for c in range(COUPLE)], axis=0)
            value = jnp.dot(near, inbufs[s][q], preferred_element_type=jnp.float32)
            if s == 0:
                acc[q] = value
            else:
                acc[q] += value

        def one(i):
            g = lax.rem(i * stride, planes)
            q = lax.rem(plane + planes - g, planes)
            dst = inbufs[s].at[q]
            pltpu.make_async_copy(dst, dst, pr.at[s, g]).wait()
            product(q)

        product(plane)
        loop(1, planes, one)

    pl.semaphore_wait(barrier, nz - 1 + planes - 1 + greeted)

    pltpu.make_async_copy(table, ztab.at[zlo], tzr.at[0]).start()
    loop(1, nz, lambda d: table_copy(d).start())
    loop(1, nz, lambda i: z_one(0, i))
    z_self(0)

    def table_wait(d):
        dst = ztab.at[lax.rem(zlo + nz - d, nz)]
        pltpu.make_async_copy(dst, dst, tzr.at[d]).wait()

    loop(0, nz, table_wait)
    pltpu.make_async_copy(ztab, xtab.at[x], txr.at[0]).start()
    loop(1, nx, lambda d: row_copy(x, d).start())

    for s in range(SPLIT):
        relay(s)
        if s == 0:
            def row_wait(d):
                dst = xtab.at[lax.rem(x + nx - d, nx)]
                pltpu.make_async_copy(dst, dst, txr.at[d]).wait()

            loop(0, nx, row_wait)
            fetch = pltpu.make_async_copy(xtab, stab, tsem)
            fetch.start()
            fetch.wait()
        pick(s)
        if s > 0:
            multiply(s - 1)
        turn(s)
    multiply(SPLIT - 1)
    reduce_over_z()

    loop(1, nz, lambda d: table_copy(d).wait_send())
    loop(1, nx, lambda d: row_copy(x, d).wait_send())
    for s in range(SPLIT):
        loop(1, nz, lambda d: z_copy(s, d).wait_send())
        loop(1, nz, lambda e: y_copy(s, e).wait_send())
        loop(1, planes, lambda g: p_copy(s, g).wait_send())


def shards(sensitivity, run_counts, req_owner, req_block, coupled):
    rows_dev, cols = sensitivity.shape
    blocks = run_counts.shape[0]
    nx, nz, nh, ny, nc = (lax.axis_size(a) for a in ("x", "zlo", "zhi", "y", "core"))
    regions = nx * nz
    runs = nh * ny * nc
    sub = [n * rows_dev // (nz * sum(PARTS)) for n in PARTS]
    vmem = pl.BlockSpec(memory_space=pltpu.VMEM)
    dma = pltpu.SemaphoreType.DMA

    fields = jnp.concatenate([req_block[:, None], coupled], axis=1)
    hit = req_owner[:, 0][:, None] == jnp.arange(regions, dtype=jnp.int32)[None, :]
    sorted_fields = jnp.sum(jnp.where(hit[:, None, :], fields[:, :, None], 0), axis=0)
    table = jnp.pad(sorted_fields, ((0, 8 - 1 - COUPLE), (0, 128 - regions)))

    share = BS // runs
    depth = nh * nz
    by_owner, by_source = pl.pallas_call(
        functools.partial(fisher_kernel, (nx, nz, nh, ny, nc)),
        out_shape=[jax.ShapeDtypeStruct((regions, COUPLE * share, BS), jnp.bfloat16)] * 2,
        in_specs=[vmem, pl.BlockSpec(memory_space=pltpu.SMEM), vmem],
        out_specs=[vmem, vmem],
        scratch_shapes=[
            pltpu.VMEM((regions, COUPLE * BS, BS), jnp.float32),
            pltpu.VMEM((2, depth // 2, 2, COUPLE * BS, BS), jnp.float32),
            pltpu.VMEM((runs, 2, COUPLE * share, BS), jnp.bfloat16),
            dma((2, depth // 2, PIECES)), dma((2, depth // 2, PIECES)),
            dma((runs,)), dma((depth,)),
            dma((2, runs)), dma((regions,)),
            pltpu.VMEM((nz, 8, 128), jnp.int32),
            pltpu.VMEM((nx, nz, 8, 128), jnp.int32),
            pltpu.SMEM((nx, nz, 8, 128), jnp.int32),
            dma((SPLIT, nz)), dma((SPLIT, nz)),
            dma((SPLIT, nz)), dma((SPLIT, nz)),
            dma((SPLIT, regions)), dma((SPLIT, regions)),
            dma((nz,)), dma((nz,)), dma((nx,)), dma((nx,)), dma,
        ] + [
            pltpu.VMEM(shape, jnp.bfloat16)
            for shape in (
                [(nz, blocks, n, BS) for n in sub] * 2
                + [(blocks, nz, n, BS) for n in sub]
                + [(blocks, BS, nz * n) for n in sub]
                + [(regions, nz * n, BS) for n in sub] * 2)
        ],
        compiler_params=pltpu.CompilerParams(
            collective_id=0, has_side_effects=True, vmem_limit_bytes=54 << 20),
    )(sensitivity, run_counts, table)

    fisher = jnp.take(by_owner, req_owner[:, 0], axis=0).reshape(-1, COUPLE, share, BS)
    mirror = jnp.swapaxes(by_source.reshape(-1, COUPLE, share, BS), 2, 3)
    return fisher, mirror.reshape(1, regions, 1, COUPLE, BS, share)


def solution(mesh):
    fine = Mesh(mesh.devices.reshape(4, 8, 2, 4, 2), ("x", "zlo", "zhi", "y", "core"))
    return build(fine)


def build(fine):
    in_specs = (P(RUN, REGION), P(REGION), P(REGION, None), P(REGION), P(REGION, None))
    out_specs = (P(REGION, None, RUN, None), P(REGION, None, None, None, None, RUN))
    return jax.shard_map(shards, mesh=fine, in_specs=in_specs, out_specs=out_specs, check_vma=False)
```

time: 300 us -> 292 us (0.973); the launches traced: 295 us -> 292 us
    unnamed x9 -> x3, local copies, waits for them, and re-layouts: 5.38 us -> 1.57 us
    pallas_call x2 -> x1, Pallas kernels: 287 us -> 285 us  [shards(): pl.pallas_call(functools.partial(fisher_kernel, (nx, nz, nh, ny, nc)), ou...]
where the time goes in v6:
time: 292 us
  Pallas kernels  285 us (98%)
  local copies, waits for them, and re-layouts  3.67 us (1%)
    pallas_call x1, Pallas kernels, shards(): pl.pallas_call(functools.partial(fisher_kernel, (nx, nz, nh, ny, nc)), ou...  285 us

profile of v6, /device:TPU:1, one launch (start us, length us, event | category | flops | bytes accessed | tf_op | source)
XLA Modules:
  0.0 291.7 jit_solution(4405971219634568798)
XLA Ops:
  0.6 0.0 copy-start
  0.6 0.8 iota_compare_fusion
  1.4 0.7 pad_add_fusion
  2.1 0.1 select_reduce_fusion
  2.2 0.6 pad.4.table
  2.8 285.0 %shard_map.68 = (bf16[32,16,128]{2,1,0:T(8,128)(2,1)}, bf16[32,16,128]{2,1,0:T(8,128)(2,1)}) custom-call(bf16[768,2048]{1,0:T(8,128)(2,1)} %sens.1, s32[16]{0:T(128)} %counts.1, s32[8,128]{1,0:T(8,128)} %pad.4.table), custom_call_target="tpu_custom_call" | custom-call | tf_op jit(solution)/shard_map/pallas_call | solution.py:444
  287.9 0.0 copy-done
  287.9 1.5 gather_fusion
  289.4 0.8 bitcast_select_fusion
  290.2 1.6 copy.9
  (3 shorter events, 0.0 us)
Async XLA Ops:
  0.6 287.2 %copy-start = (s32[32,1]{0,1:T(1,128)S(1)}, s32[32,1]{0,1:T(1,128)}, u32[]{:S(2)}) copy-start(s32[32,1]{0,1:T(1,128)} %param.7) | copy-start | bytes 388

commit v7 on v6

--- a/solution.py
+++ b/solution.py
@@ -132,13 +132,27 @@
 
     ways = [way for way in range(2) if ahead[way] > 0]
     both = max(0, ahead[1] - 1)
-    def run():
-        for p in range(len(pieces)):
+    def run(finish):
+        def complete(b):
+            for e in range(2):
+                finish(2 * b + e)
+
+        def start_of(way):
+            return lax.rem(z + depth + (ahead[0] if way == 0 else -ahead[1]), depth)
+
+        for way in ways:
+            complete(start_of(way))
+            for p in range(len(pieces)):
+                first(way, p).start()
+        def next_step(i, ways):
             for way in ways:
-                first(way, p).start()
-        loop(0, both, lambda i: step(i, [0, 1]))
+                complete(chunk(way, i))
+            step(i, ways)
+
+        loop(0, both, lambda i: next_step(i, [0, 1]))
         for i in range(both, ahead[0] - 1):
-            step(i, [0])
+            next_step(i, [0])
+        complete(z)
         for way in ways:
             for p in range(len(pieces)):
                 arrive(way, ahead[way] - 1, p)
@@ -225,8 +239,8 @@
 
 
 def fisher_kernel(
-    sizes, sens, counts, table, fbuf, mbuf, acc, ring, fin, rs, rr, fs, fr, ms, mr,
-    ztab, xtab, stab, zs, zr, ys, yr, ps, pr, tzs, tzr, txs, txr, tsem, *bufs,
+    sizes, shard, counts, table, fbuf, mbuf, acc, ring, fin, rs, rr, fs, fr, ms, mr,
+    sens, ztab, xtab, stab, zs, zr, ys, yr, ps, pr, tzs, tzr, txs, txr, tsem, *bufs,
 ):
     masked, zbufs, tbufs, turned, outbufs, inbufs = (
         bufs[i * SPLIT:(i + 1) * SPLIT] for i in range(6))
@@ -258,6 +272,8 @@
     barrier = pltpu.get_barrier_semaphore()
     greet_all, greeted, reduce_over_z = reduction(
         sizes, barrier, acc, fbuf, mbuf, ring, fin, rs, rr, fs, fr, ms, mr)
+    load = pltpu.make_async_copy(shard, sens, tsem)
+    load.start()
     greet_all()
     loop(1, nz, lambda d: pl.semaphore_signal(barrier, inc=1, device_id=z_at(d), device_id_type=MESH))
     loop(1, planes, lambda g: pl.semaphore_signal(
@@ -289,8 +305,6 @@
             value = sens[pl.ds(start, sub[s]), b * BS:(b + 1) * BS].astype(jnp.float32)
             masked[s][j, b] = jnp.where(run < counts[b], value, 0.0).astype(jnp.bfloat16)
 
-    early = min(nz // 2, nz - 1)
-
     def z_self(s):
         mask(zlo, s)
         pltpu.make_async_copy(masked[s].at[zlo], zbufs[s].at[zlo], zr.at[s, 0]).start()
@@ -318,14 +332,14 @@
             def _():
                 y_copy(s, e).start()
 
-        if s + 1 < SPLIT:
+        if s + 2 < SPLIT:
             def both(i):
                 one(i)
-                z_one(s + 1, i + 1)
-
-            loop(0, early, both)
-            loop(early, nz, one)
-            z_self(s + 1)
+                z_one(s + 2, i + 1)
+
+            loop(0, nz - 1, both)
+            one(nz - 1)
+            z_self(s + 2)
         else:
             loop(0, nz, one)
 
@@ -347,14 +361,7 @@
             outbufs[s][g] = block(s, asked(lax.rem(plane + g, planes)))
             p_copy(s, g).start()
 
-        groups = nz - 1 - early if s + 1 < SPLIT else 0
-        begin = 1
-        for j in range(groups):
-            end = 1 + (planes - 1) * (j + 1) // (groups + 1)
-            loop(begin, end, one)
-            z_one(s + 1, early + 1 + j)
-            begin = end
-        loop(begin, planes, one)
+        loop(1, planes, one)
         inbufs[s][plane] = block(s, asked(plane))
 
     def turn(s):
@@ -363,32 +370,37 @@
 
         loop(0, blocks, one)
 
+    def product(s, q):
+        g = lax.rem(plane + planes - q, planes)
+
+        @pl.when(g > 0)
+        def _():
+            dst = inbufs[s].at[q]
+            pltpu.make_async_copy(dst, dst, pr.at[s, g]).wait()
+
+        near = jnp.concatenate(
+            [turned[s][stab[x, rho, 1 + c, q]] for c in range(COUPLE)], axis=0)
+        value = jnp.dot(near, inbufs[s][q], preferred_element_type=jnp.float32)
+        if s == 0:
+            acc[q] = value
+        else:
+            acc[q] += value
+
     def multiply(s):
-        def product(q):
-            near = jnp.concatenate(
-                [turned[s][stab[x, rho, 1 + c, q]] for c in range(COUPLE)], axis=0)
-            value = jnp.dot(near, inbufs[s][q], preferred_element_type=jnp.float32)
-            if s == 0:
-                acc[q] = value
-            else:
-                acc[q] += value
-
         def one(i):
             g = lax.rem(i * stride, planes)
-            q = lax.rem(plane + planes - g, planes)
-            dst = inbufs[s].at[q]
-            pltpu.make_async_copy(dst, dst, pr.at[s, g]).wait()
-            product(q)
-
-        product(plane)
-        loop(1, planes, one)
-
+            product(s, lax.rem(plane + planes - g, planes))
+
+        loop(0, planes, one)
+
+    load.wait()
     pl.semaphore_wait(barrier, nz - 1 + planes - 1 + greeted)
 
     pltpu.make_async_copy(table, ztab.at[zlo], tzr.at[0]).start()
     loop(1, nz, lambda d: table_copy(d).start())
-    loop(1, nz, lambda i: z_one(0, i))
-    z_self(0)
+    for s in range(2):
+        loop(1, nz, lambda i: z_one(s, i))
+        z_self(s)
 
     def table_wait(d):
         dst = ztab.at[lax.rem(zlo + nz - d, nz)]
@@ -413,8 +425,7 @@
         if s > 0:
             multiply(s - 1)
         turn(s)
-    multiply(SPLIT - 1)
-    reduce_over_z()
+    reduce_over_z(functools.partial(product, SPLIT - 1))
 
     loop(1, nz, lambda d: table_copy(d).wait_send())
     loop(1, nx, lambda d: row_copy(x, d).wait_send())
@@ -444,7 +455,7 @@
     by_owner, by_source = pl.pallas_call(
         functools.partial(fisher_kernel, (nx, nz, nh, ny, nc)),
         out_shape=[jax.ShapeDtypeStruct((regions, COUPLE * share, BS), jnp.bfloat16)] * 2,
-        in_specs=[vmem, pl.BlockSpec(memory_space=pltpu.SMEM), vmem],
+        in_specs=[pl.BlockSpec(memory_space=pl.ANY), pl.BlockSpec(memory_space=pltpu.SMEM), vmem],
         out_specs=[vmem, vmem],
         scratch_shapes=[
             pltpu.VMEM((regions, COUPLE * BS, BS), jnp.float32),
@@ -453,6 +464,7 @@
             dma((2, depth // 2, PIECES)), dma((2, depth // 2, PIECES)),
             dma((runs,)), dma((depth,)),
             dma((2, runs)), dma((regions,)),
+            pltpu.VMEM((rows_dev, cols), jnp.bfloat16),
             pltpu.VMEM((nz, 8, 128), jnp.int32),
             pltpu.VMEM((nx, nz, 8, 128), jnp.int32),
             pltpu.SMEM((nx, nz, 8, 128), jnp.int32),

time: 292 us -> 307 us (1.051)
  Pallas kernels: 285 us -> 298 us
    pallas_call x1, Pallas kernels: 285 us -> 298 us  [shards(): pl.pallas_call(functools.partial(fisher_kernel, (nx, nz, nh, ny, nc)), ou...]
where the time goes in v7:
time: 307 us; the launch traced here: 305 us
  Pallas kernels  298 us (97%)
  local copies, waits for them, and re-layouts  3.67 us (1%)
    pallas_call x1, Pallas kernels, shards(): pl.pallas_call(functools.partial(fisher_kernel, (nx, nz, nh, ny, nc)), ou...  298 us

profile of v7, /device:TPU:1, one launch (start us, length us, event | category | flops | bytes accessed | tf_op | source)
XLA Modules:
  0.0 304.6 jit_solution(3189257696866952083)
XLA Ops:
  0.6 0.0 copy-start
  0.6 0.8 iota_compare_fusion
  1.4 0.7 pad_add_fusion
  2.1 0.1 select_reduce_fusion
  2.2 0.6 pad.4.table
  2.8 297.8 %shard_map.68 = (bf16[32,16,128]{2,1,0:T(8,128)(2,1)}, bf16[32,16,128]{2,1,0:T(8,128)(2,1)}) custom-call(bf16[768,2048]{1,0:T(8,128)(2,1)} %shard.1, s32[16]{0:T(128)} %counts.1, s32[8,128]{1,0:T(8,128)} %pad.4.table), custom_call_target="tpu_custom_call" | custom-call | tf_op jit(solution)/shard_map/pallas_call | solution.py:455
  300.7 0.0 copy-done
  300.7 1.5 gather_fusion
  302.2 0.8 bitcast_select_fusion
  303.0 1.6 copy.9
  (3 shorter events, 0.0 us)
Async XLA Ops:
  0.6 300.0 %copy-start = (s32[32,1]{0,1:T(1,128)S(1)}, s32[32,1]{0,1:T(1,128)}, u32[]{:S(2)}) copy-start(s32[32,1]{0,1:T(1,128)} %param.7) | copy-start | bytes 388

commit v8 on v7

--- a/solution.py
+++ b/solution.py
@@ -305,6 +305,8 @@
             value = sens[pl.ds(start, sub[s]), b * BS:(b + 1) * BS].astype(jnp.float32)
             masked[s][j, b] = jnp.where(run < counts[b], value, 0.0).astype(jnp.bfloat16)
 
+    early = min(nz // 2, nz - 1)
+
     def z_self(s):
         mask(zlo, s)
         pltpu.make_async_copy(masked[s].at[zlo], zbufs[s].at[zlo], zr.at[s, 0]).start()
@@ -332,14 +334,14 @@
             def _():
                 y_copy(s, e).start()
 
-        if s + 2 < SPLIT:
+        if s + 1 < SPLIT:
             def both(i):
                 one(i)
-                z_one(s + 2, i + 1)
-
-            loop(0, nz - 1, both)
-            one(nz - 1)
-            z_self(s + 2)
+                z_one(s + 1, i + 1)
+
+            loop(0, early, both)
+            loop(early, nz, one)
+            z_self(s + 1)
         else:
             loop(0, nz, one)
 
@@ -361,7 +363,14 @@
             outbufs[s][g] = block(s, asked(lax.rem(plane + g, planes)))
             p_copy(s, g).start()
 
-        loop(1, planes, one)
+        groups = nz - 1 - early if s + 1 < SPLIT else 0
+        begin = 1
+        for j in range(groups):
+            end = 1 + (planes - 1) * (j + 1) // (groups + 1)
+            loop(begin, end, one)
+            z_one(s + 1, early + 1 + j)
+            begin = end
+        loop(begin, planes, one)
         inbufs[s][plane] = block(s, asked(plane))
 
     def turn(s):
@@ -398,9 +407,8 @@
 
     pltpu.make_async_copy(table, ztab.at[zlo], tzr.at[0]).start()
     loop(1, nz, lambda d: table_copy(d).start())
-    for s in range(2):
-        loop(1, nz, lambda i: z_one(s, i))
-        z_self(s)
+    loop(1, nz, lambda i: z_one(0, i))
+    z_self(0)
 
     def table_wait(d):
         dst = ztab.at[lax.rem(zlo + nz - d, nz)]

time: 307 us -> 285 us (0.928)
  Pallas kernels: 298 us -> 273 us
    pallas_call x1, Pallas kernels: 298 us -> 273 us  [shards(): pl.pallas_call(functools.partial(fisher_kernel, (nx, nz, nh, ny, nc)), ou...]
where the time goes in v8:
time: 285 us; the launch traced here: 280 us
  Pallas kernels  273 us (96%)
  local copies, waits for them, and re-layouts  3.67 us (1%)
    pallas_call x1, Pallas kernels, shards(): pl.pallas_call(functools.partial(fisher_kernel, (nx, nz, nh, ny, nc)), ou...  273 us

profile of v8, /device:TPU:1, one launch (start us, length us, event | category | flops | bytes accessed | tf_op | source)
XLA Modules:
  0.0 280.0 jit_solution(9081950486052453320)
XLA Ops:
  0.6 0.0 copy-start
  0.6 0.8 iota_compare_fusion
  1.4 0.7 pad_add_fusion
  2.1 0.1 select_reduce_fusion
  2.2 0.6 pad.4.table
  2.8 273.3 %shard_map.68 = (bf16[32,16,128]{2,1,0:T(8,128)(2,1)}, bf16[32,16,128]{2,1,0:T(8,128)(2,1)}) custom-call(bf16[768,2048]{1,0:T(8,128)(2,1)} %shard.1, s32[16]{0:T(128)} %counts.1, s32[8,128]{1,0:T(8,128)} %pad.4.table), custom_call_target="tpu_custom_call" | custom-call | tf_op jit(solution)/shard_map/pallas_call | solution.py:463
  276.1 0.0 copy-done
  276.2 1.5 gather_fusion
  277.7 0.8 bitcast_select_fusion
  278.4 1.6 copy.9
  (3 shorter events, 0.0 us)
Async XLA Ops:
  0.6 275.5 %copy-start = (s32[32,1]{0,1:T(1,128)S(1)}, s32[32,1]{0,1:T(1,128)}, u32[]{:S(2)}) copy-start(s32[32,1]{0,1:T(1,128)} %param.7) | copy-start | bytes 388
